TPU v7x, 256 devices: a whole 4x4x8 slice. The times are simulated.
256 devices in a mesh: section: 8 (over y, core), expert: 32 (over z, x).
Axes of the slice: x: 4, y: 4, z: 8, core: 2. Of those that a mesh axis runs over, the one named last changes fastest.
Arguments:
- tokens: bfloat16 [4096, 7168], P('expert', 'section'), may hold values from -6 to 6
- routes: int32 [4096, 8], P('expert'), may hold values from 0 to 63, all different within a row; in each aligned block of 128 rows (0 to 127, 128 to 255, ...) at most 24 rows name the same one
- combine: float32 [4096, 8], P('expert'), may hold values from 0.05 to 0.6
- gate_weight: bfloat16 [64, 7168, 1024], P('expert', 'section'), may hold values from -0.0625 to 0.0625
- up_weight: bfloat16 [64, 7168, 1024], P('expert', 'section'), may hold values from -0.0625 to 0.0625
- down_weight: bfloat16 [64, 1024, 7168], P('expert', None, 'section'), may hold values from -0.1875 to 0.1875
Outputs:
- mixed: bfloat16 [4096, 7168], P('expert', 'section')
Inputs may be any that keep to these rules, and one draw needn't show every extreme that they name: `routes`: among the 128 rows of one block of tokens, no expert is named more than 24 times; in every draw some expert is named exactly 24 times in some block. The 8 experts of a token differ.
All inputs are finite; a program needn't handle non-finite values.
Results may differ from a plain program's by a relative error of at most 0.029.
Values may be sent and summed in bfloat16 or wider, within the bound.
No kernel may reach another device: no remote copies, remote signals or barrier semaphores. Data moves between devices by JAX's collectives and lax.ppermute only.
A program may use at most 64 MiB of HBM per device.

v0:
```python
import functools

import jax
import jax.numpy as jnp
from jax import lax
from jax.experimental import pallas as pl
from jax.experimental.pallas import tpu as pltpu
from jax.sharding import PartitionSpec as P

BF16, F32 = jnp.bfloat16, jnp.float32
NX, CORES = 4, 2
CHUNKS = ((1, -1, 2, -2), (0, 4, 3, -3))
VMEM = pl.BlockSpec(memory_space=pltpu.VMEM)
SMEM = pl.BlockSpec(memory_space=pltpu.SMEM)


def along_expert(value, dz, dx):
    count = lax.axis_size("expert")
    planes = count // NX
    return lax.ppermute(
        value,
        "expert",
        [(i, (i // NX + dz) % planes * NX + (i % NX + dx) % NX) for i in range(count)],
    )


def along_section(value, dy, flip):
    count = lax.axis_size("section")
    return lax.ppermute(
        value, "section", [(i, (i + CORES * dy) % count ^ flip) for i in range(count)]
    )


def call(kernel, outs, specs=None, grid=(), out_specs=None, scratch=(), limit=24, flops=0, moved=0):
    return pl.pallas_call(
        kernel,
        grid=grid,
        out_shape=outs,
        in_specs=specs,
        out_specs=out_specs or jax.tree.map(lambda _: VMEM, outs),
        scratch_shapes=scratch,
        compiler_params=pltpu.CompilerParams(vmem_limit_bytes=limit << 20),
        cost_estimate=pl.CostEstimate(flops=flops, bytes_accessed=moved, transcendentals=0),
    )


def select_kernel(capacity, rows, at_ref, *refs):
    nz = len(refs) - 6
    blocks, outs, code_ref, weight_ref = refs[:nz], refs[nz : nz + 4], refs[-2], refs[-1]
    per_plane = 2 * NX
    row = lax.broadcasted_iota(jnp.int32, (per_plane, rows), 0)
    expert = (at_ref[0] * per_plane + (at_ref[1] + row // 2) % NX * 2 + row % 2).astype(F32)
    earlier = (
        lax.broadcasted_iota(jnp.int32, (rows, rows), 0)
        < lax.broadcasted_iota(jnp.int32, (rows, rows), 1)
    ).astype(F32).astype(BF16)
    codes = []
    for n, block in enumerate(blocks):
        info = block[pl.ds(rows, 16), pl.ds(0, rows)].astype(F32)
        named = jnp.zeros((per_plane, rows), F32)
        weight = jnp.zeros((per_plane, rows), F32)
        for k in range(8):
            hit = info[k : k + 1] == expert
            named = named + jnp.where(hit, 1.0, 0.0)
            weight = weight + jnp.where(hit, info[8 + k : 9 + k], 0.0)
        slot = jnp.dot(named.astype(BF16), earlier, preferred_element_type=F32)
        codes.append(jnp.where(named > 0.5, slot + float(n * capacity), -1.0))
        weight_ref[:, pl.ds(n * rows, rows)] = weight
    code = jnp.concatenate(codes, axis=1)
    code_ref[...] = code
    held = nz * capacity
    at = lax.broadcasted_iota(jnp.int32, (held, nz * rows), 0).astype(F32)
    tokens = jnp.concatenate([block[pl.ds(0, rows), :] for block in blocks], axis=0)
    for r in range(NX):
        pick = jnp.concatenate(
            [jnp.where(at == code[2 * r + e : 2 * r + e + 1], 1.0, 0.0) for e in range(2)], axis=0
        ).astype(BF16)
        outs[r][...] = jnp.dot(pick, tokens, preferred_element_type=F32).astype(BF16)


def up_kernel(held, at_ref, *refs):
    rows, gate_ref, up_ref, keep_ref, send_ref, x_ref = refs[:4], *refs[4:]
    core, y = at_ref[3], at_ref[2]

    @pl.when(pl.program_id(0) == 0)
    def _():
        for r in range(4):
            for e in range(2):
                x_ref[e, pl.ds(r * held, held), :] = rows[r][pl.ds(e * held, held), :]

    for out_ref, e in ((keep_ref, core), (send_ref, 1 - core)):
        x = x_ref[e]
        for part, weight_ref in enumerate((gate_ref, up_ref)):
            sums = jnp.dot(x, weight_ref[e], preferred_element_type=F32).astype(BF16)
            for r in range(4):
                out_ref[(r + 4 - y) % 4, part] = sums[r * held : (r + 1) * held]


def join_kernel(keep_ref, got_ref, *outs):
    for q in range(4):
        outs[q][...] = (keep_ref[q].astype(F32) + got_ref[q].astype(F32)).astype(BF16)


def silu_kernel(a_ref, b_ref, c_ref, d_ref, out_ref):
    gate, up = (
        (a_ref[i].astype(F32) + b_ref[i].astype(F32)) + (c_ref[i].astype(F32) + d_ref[i].astype(F32))
        for i in range(2)
    )
    out_ref[...] = (jax.nn.silu(gate) * up).astype(BF16)


def down_kernel(held, at_ref, *refs):
    parts, down_ref, outs, h_ref = refs[:2], refs[2], refs[3:7], refs[7]
    core, y = at_ref[3], at_ref[2]

    @pl.when(pl.program_id(0) == 0)
    def _():
        for q in range(4):
            for f in range(2):
                at = pl.multiple_of((y + 4 - q) % 4 * held, held)
                h_ref[(core + f) % 2, pl.ds(at, held), :] = parts[f][q]

    got = jnp.dot(h_ref[pl.program_id(0)], down_ref[0], preferred_element_type=F32).astype(BF16)
    for r in range(4):
        outs[r][...] = got[r * held : (r + 1) * held]


def mix_kernel(held, rows, a_ref, b_ref, c_ref, d_ref, code_ref, weight_ref, *outs):
    width = code_ref.shape[1]
    at = lax.broadcasted_iota(jnp.int32, (held, width), 0).astype(F32)
    share = jnp.concatenate(
        [
            jnp.where(at == code_ref[j : j + 1, :], weight_ref[j : j + 1, :], 0.0)
            for j in range(2 * NX)
        ],
        axis=0,
    ).astype(BF16)
    back = jnp.concatenate([ref[...] for ref in (a_ref, b_ref, c_ref, d_ref)], axis=0)
    total = lax.dot_general(
        share, back, (((0,), (0,)), ((), ())), preferred_element_type=F32
    ).astype(BF16)
    for n, out in enumerate(outs):
        out[...] = total[n * rows : (n + 1) * rows]


def shape(*dims, dtype=BF16):
    return jax.ShapeDtypeStruct(dims, dtype)


def body(tokens, routes, combine, gate_weight, up_weight, down_weight):
    groups = lax.axis_size("expert")
    per_device, width, units = gate_weight.shape
    rows, fanout = routes.shape
    capacity = 3 * rows * fanout // (2 * per_device * groups)
    place, part = lax.axis_index("expert"), lax.axis_index("section")
    at = jnp.stack([place // NX, place % NX, part // CORES, part % CORES]).astype(jnp.int32)

    info = jnp.concatenate([routes.T.astype(BF16), combine.T.astype(BF16)], axis=0)
    message = jnp.concatenate([tokens, jnp.pad(info, ((0, 0), (0, width - rows)))], axis=0)

    partials = []
    blocks = ()
    for chunk in CHUNKS:
        nz = len(chunk)
        held = nz * capacity
        sent, _ = lax.optimization_barrier((message, blocks))
        blocks = [along_expert(sent, d, 0) if d else sent for d in chunk]
        *picked, code, weight = call(
            functools.partial(select_kernel, capacity, rows),
            [shape(2 * held, width)] * 4 + [shape(2 * NX, nz * rows, dtype=F32)] * 2,
            [SMEM] + [VMEM] * nz,
            flops=16 * held * nz * rows * width,
            moved=2 << 20,
        )(at, *blocks)
        came = [along_expert(picked[r], 0, r) if r else picked[r] for r in range(4)]
        tile = 256
        whole = lambda i: (0, 0)
        keep, send = call(
            functools.partial(up_kernel, held),
            [shape(4, 2, held, units)] * 2,
            [SMEM]
            + [pl.BlockSpec((2 * held, width), whole)] * 4
            + [pl.BlockSpec((2, width, tile), lambda i: (0, 0, i))] * 2,
            grid=(units // tile,),
            out_specs=[pl.BlockSpec((4, 2, held, tile), lambda i: (0, 0, 0, i))] * 2,
            scratch=[pltpu.VMEM((2, 4 * held, width), BF16)],
            flops=32 * held * width * units,
            moved=10 << 20,
        )(at, *came, gate_weight, up_weight)
        got = along_section(send, 0, 1)
        sums = call(
            join_kernel, [shape(2, held, units)] * 4, [VMEM] * 2, moved=3 << 20
        )(keep, got)
        terms = [along_section(sums[q], q, 0) if q else sums[q] for q in range(4)]
        hidden = call(silu_kernel, shape(held, units), [VMEM] * 4, moved=1 << 20)(*terms)
        parts = jnp.stack([along_section(hidden, q, 0) if q else hidden for q in range(4)])
        others = along_section(parts, 0, 1)
        out = call(
            functools.partial(down_kernel, held),
            [shape(2 * held, width)] * 4,
            [SMEM]
            + [pl.BlockSpec((4, held, units), lambda i: (0, 0, 0))] * 2
            + [pl.BlockSpec((1, units, width), lambda i: (i, 0, 0))],
            grid=(2,),
            out_specs=[pl.BlockSpec((held, width), lambda i: (i, 0))] * 4,
            scratch=[pltpu.VMEM((2, 4 * held, units), BF16)],
            flops=16 * held * width * units,
            moved=6 << 20,
        )(at, parts, others, down_weight)
        back = [along_expert(out[r], 0, -r) if r else out[r] for r in range(4)]
        mixed = call(
            functools.partial(mix_kernel, held, rows),
            [shape(rows, width)] * nz,
            [VMEM] * 6,
            flops=16 * held * nz * rows * width,
            moved=2 << 20,
        )(*back, code, weight)
        partials += [along_expert(m, -d, 0) if d else m for d, m in zip(chunk, mixed)]
    return sum(p.astype(F32) for p in partials).astype(BF16)


def solution(mesh):
    return jax.shard_map(
        body,
        mesh=mesh,
        in_specs=(
            P("expert", "section"),
            P("expert", None),
            P("expert", None),
            P("expert", "section", None),
            P("expert", "section", None),
            P("expert", None, "section"),
        ),
        out_specs=P("expert", "section"),
        check_vma=False,
    )
```

profile of v0, /device:TPU:6, one launch (start us, length us, event | category | flops | bytes accessed | tf_op | source)
XLA Modules:
  0.0 241.6 jit_solution(6159890124474503778)
XLA Ops:
  4.3 4.0 %collective-permute-start.1 = (bf16[144,896]{1,0:T(8,128)(2,1)S(1)}, bf16[144,896]{1,0:T(8,128)(2,1)S(1)}, u32[]{:S(2)}, u32[]{:S(2)}) collective-permute-start(bf16[144,896]{1,0:T(8,128)(2,1)S(1)} %pad_maximum_fusion.2.refs_0_), channel_id=1, source_target_pairs={{0,28},{1,29},{2,30},{3,31},{4,0},{5,1},{6,2},{7,3},{8,4},{9,5},{1... | collective-permute-start | bytes 774152 | tf_op jit(solution)/shard_map/ppermute | solution.py:20
  8.4 4.1 %collective-permute-start.3 = (bf16[144,896]{1,0:T(8,128)(2,1)S(1)}, bf16[144,896]{1,0:T(8,128)(2,1)S(1)}, u32[]{:S(2)}, u32[]{:S(2)}) collective-permute-start(bf16[144,896]{1,0:T(8,128)(2,1)S(1)} %pad_maximum_fusion.2.refs_0_), channel_id=1, source_target_pairs={{0,24},{1,25},{2,26},{3,27},{4,28},{5,29},{6,30},{7,31},{8,0},{9,1... | collective-permute-start | bytes 774152 | tf_op jit(solution)/shard_map/ppermute | solution.py:20
  15.8 4.6 %collective-permute-done.1.refs_1_ = bf16[144,896]{1,0:T(8,128)(2,1)S(1)} collective-permute-done((bf16[144,896]{1,0:T(8,128)(2,1)S(1)}, bf16[144,896]{1,0:T(8,128)(2,1)S(1)}, u32[]{:S(2)}, u32[]{:S(2)}) %collective-permute-start.1) | collective-permute-done | bytes 258080 | tf_op jit(solution)/shard_map/ppermute | solution.py:20
  24.9 4.9 %collective-permute-start.22 = (bf16[144,896]{1,0:T(8,128)(2,1)S(1)}, bf16[144,896]{1,0:T(8,128)(2,1)S(1)}, u32[]{:S(2)}, u32[]{:S(2)}) collective-permute-start(bf16[144,896]{1,0:T(8,128)(2,1)S(1)} %pad_maximum_fusion.2.refs_0_), channel_id=1, source_target_pairs={{0,16},{1,17},{2,18},{3,19},{4,20},{5,21},{6,22},{7,23},{8,24},{9,... | collective-permute-start | bytes 774152 | tf_op jit(solution)/shard_map/ppermute | solution.py:20
  36.0 10.1 %collective-permute-start.24 = (bf16[144,896]{1,0:T(8,128)(2,1)S(1)}, bf16[144,896]{1,0:T(8,128)(2,1)S(1)}, u32[]{:S(2)}, u32[]{:S(2)}) collective-permute-start(bf16[144,896]{1,0:T(8,128)(2,1)S(1)} %pad_maximum_fusion.2.refs_0_), channel_id=1, source_target_pairs={{0,20},{1,21},{2,22},{3,23},{4,24},{5,25},{6,26},{7,27},{8,28},{9,... | collective-permute-start | bytes 774152 | tf_op jit(solution)/shard_map/ppermute | solution.py:20
  46.2 11.0 %collective-permute-done.23.refs_2_ = bf16[144,896]{1,0:T(8,128)(2,1)S(1)} collective-permute-done((bf16[144,896]{1,0:T(8,128)(2,1)S(1)}, bf16[144,896]{1,0:T(8,128)(2,1)S(1)}, u32[]{:S(2)}, u32[]{:S(2)}) %collective-permute-start.23) | collective-permute-done | bytes 258080 | tf_op jit(solution)/shard_map/ppermute | solution.py:20
  57.2 5.7 %collective-permute-done.24.refs_3_ = bf16[144,896]{1,0:T(8,128)(2,1)S(1)} collective-permute-done((bf16[144,896]{1,0:T(8,128)(2,1)S(1)}, bf16[144,896]{1,0:T(8,128)(2,1)S(1)}, u32[]{:S(2)}, u32[]{:S(2)}) %collective-permute-start.24) | collective-permute-done | bytes 258080 | tf_op jit(solution)/shard_map/ppermute | solution.py:20
  69.9 5.9 %shard_map.65 = (bf16[4,2,96,1024]{3,2,1,0:T(8,128)(2,1)S(1)}, bf16[4,2,96,1024]{3,2,1,0:T(8,128)(2,1)S(1)}) custom-call(s32[4]{0:T(128)S(1)} %pad_add_fusion.at_ref, bf16[192,896]{1,0:T(8,128)(2,1)S(1)} %get-tuple-element.46.refs_0_, bf16[192,896]{1,0:T(8,128)(2,1)S(1)} %collective-permute-done.4.refs_1_, ...), custom_call_target="tpu_custom_call" | custom-call | flops 2818572288 | bytes 10485760 | tf_op jit(solution)/shard_map/pallas_call | solution.py:178
  77.5 5.1 %collective-permute-done.27.refs_3_ = bf16[192,896]{1,0:T(8,128)(2,1)S(1)} collective-permute-done((bf16[192,896]{1,0:T(8,128)(2,1)S(1)}, bf16[192,896]{1,0:T(8,128)(2,1)S(1)}, u32[]{:S(2)}, u32[]{:S(2)}) %collective-permute-start.27) | collective-permute-done | bytes 344096 | tf_op jit(solution)/shard_map/ppermute | solution.py:20
  82.6 5.9 %shard_map.71 = (bf16[4,2,96,1024]{3,2,1,0:T(8,128)(2,1)S(1)}, bf16[4,2,96,1024]{3,2,1,0:T(8,128)(2,1)S(1)}) custom-call(s32[4]{0:T(128)S(1)} %pad_add_fusion.at_ref, bf16[192,896]{1,0:T(8,128)(2,1)S(1)} %get-tuple-element.67.refs_0_, bf16[192,896]{1,0:T(8,128)(2,1)S(1)} %collective-permute-done.25.refs_1_, ...), custom_call_target="tpu_custom_call" | custom-call | flops 2818572288 | bytes 10485760 | tf_op jit(solution)/shard_map/pallas_call | solution.py:178
  94.9 7.0 %collective-permute-done.8.b_ref = bf16[2,96,1024]{2,1,0:T(8,128)(2,1)S(1)} collective-permute-done((bf16[2,96,1024]{2,1,0:T(8,128)(2,1)S(1)}, bf16[2,96,1024]{2,1,0:T(8,128)(2,1)S(1)}, u32[]{:S(2)}, u32[]{:S(2)}) %collective-permute-start.8) | collective-permute-done | bytes 393248 | tf_op jit(solution)/shard_map/ppermute | solution.py:29
  101.9 9.6 %collective-permute-done.9.c_ref = bf16[2,96,1024]{2,1,0:T(8,128)(2,1)S(1)} collective-permute-done((bf16[2,96,1024]{2,1,0:T(8,128)(2,1)S(1)}, bf16[2,96,1024]{2,1,0:T(8,128)(2,1)S(1)}, u32[]{:S(2)}, u32[]{:S(2)}) %collective-permute-start.9) | collective-permute-done | bytes 393248 | tf_op jit(solution)/shard_map/ppermute | solution.py:29
  120.6 6.8 %collective-permute-done.13 = bf16[96,1024]{1,0:T(8,128)(2,1)S(1)} collective-permute-done((bf16[96,1024]{1,0:T(8,128)(2,1)S(1)}, bf16[96,1024]{1,0:T(8,128)(2,1)S(1)}, u32[]{:S(2)}, u32[]{:S(2)}) %collective-permute-start.13) | collective-permute-done | bytes 196640 | tf_op jit(solution)/shard_map/ppermute | solution.py:29
  127.3 12.2 %collective-permute-done.12 = bf16[96,1024]{1,0:T(8,128)(2,1)S(1)} collective-permute-done((bf16[96,1024]{1,0:T(8,128)(2,1)S(1)}, bf16[96,1024]{1,0:T(8,128)(2,1)S(1)}, u32[]{:S(2)}, u32[]{:S(2)}) %collective-permute-start.12) | collective-permute-done | bytes 196640 | tf_op jit(solution)/shard_map/ppermute | solution.py:29
  139.6 3.7 %collective-permute-done.11 = bf16[96,1024]{1,0:T(8,128)(2,1)S(1)} collective-permute-done((bf16[96,1024]{1,0:T(8,128)(2,1)S(1)}, bf16[96,1024]{1,0:T(8,128)(2,1)S(1)}, u32[]{:S(2)}, u32[]{:S(2)}) %collective-permute-start.11) | collective-permute-done | bytes 196640 | tf_op jit(solution)/shard_map/ppermute | solution.py:29
  143.7 10.1 %collective-permute-start.34 = (bf16[96,1024]{1,0:T(8,128)(2,1)S(1)}, bf16[96,1024]{1,0:T(8,128)(2,1)S(1)}, u32[]{:S(2)}, u32[]{:S(2)}) collective-permute-start(bf16[96,1024]{1,0:T(8,128)(2,1)S(1)} %shard_map.73), channel_id=1, source_target_pairs={{0,192},{32,224},{64,0},{96,32},{128,64},{160,96},{192,128},{224,1... | collective-permute-start | bytes 589832 | tf_op jit(solution)/shard_map/ppermute | solution.py:29
  155.8 5.7 %collective-permute-done.34 = bf16[96,1024]{1,0:T(8,128)(2,1)S(1)} collective-permute-done((bf16[96,1024]{1,0:T(8,128)(2,1)S(1)}, bf16[96,1024]{1,0:T(8,128)(2,1)S(1)}, u32[]{:S(2)}, u32[]{:S(2)}) %collective-permute-start.34) | collective-permute-done | bytes 196640 | tf_op jit(solution)/shard_map/ppermute | solution.py:29
  163.2 3.8 %collective-permute-done.32 = bf16[96,1024]{1,0:T(8,128)(2,1)S(1)} collective-permute-done((bf16[96,1024]{1,0:T(8,128)(2,1)S(1)}, bf16[96,1024]{1,0:T(8,128)(2,1)S(1)}, u32[]{:S(2)}, u32[]{:S(2)}) %collective-permute-start.32) | collective-permute-done | bytes 196640 | tf_op jit(solution)/shard_map/ppermute | solution.py:29
  179.3 10.1 %collective-permute-done.15.b_ref = bf16[192,896]{1,0:T(8,128)(2,1)S(1)} collective-permute-done((bf16[192,896]{1,0:T(8,128)(2,1)S(1)}, bf16[192,896]{1,0:T(8,128)(2,1)S(1)}, u32[]{:S(2)}, u32[]{:S(2)}) %collective-permute-start.15) | collective-permute-done | bytes 344096 | tf_op jit(solution)/shard_map/ppermute | solution.py:20
  195.5 8.1 %collective-permute-done.36.b_ref = bf16[192,896]{1,0:T(8,128)(2,1)S(1)} collective-permute-done((bf16[192,896]{1,0:T(8,128)(2,1)S(1)}, bf16[192,896]{1,0:T(8,128)(2,1)S(1)}, u32[]{:S(2)}, u32[]{:S(2)}) %collective-permute-start.36) | collective-permute-done | bytes 344096 | tf_op jit(solution)/shard_map/ppermute | solution.py:20
  209.0 4.1 %collective-permute-start.40 = (bf16[128,896]{1,0:T(8,128)(2,1)S(1)}, bf16[128,896]{1,0:T(8,128)(2,1)S(1)}, u32[]{:S(2)}, u32[]{:S(2)}) collective-permute-start(bf16[128,896]{1,0:T(8,128)(2,1)S(1)} %get-tuple-element.85), channel_id=1, source_target_pairs={{0,20},{1,21},{2,22},{3,23},{4,24},{5,25},{6,26},{7,27},{8,28},{9,... | collective-permute-start | bytes 688136 | tf_op jit(solution)/shard_map/ppermute | solution.py:20
  213.1 3.9 %collective-permute-start.39 = (bf16[128,896]{1,0:T(8,128)(2,1)S(1)}, bf16[128,896]{1,0:T(8,128)(2,1)S(1)}, u32[]{:S(2)}, u32[]{:S(2)}) collective-permute-start(bf16[128,896]{1,0:T(8,128)(2,1)S(1)} %get-tuple-element.84), channel_id=1, source_target_pairs={{0,16},{1,17},{2,18},{3,19},{4,20},{5,21},{6,22},{7,23},{8,24},{9,... | collective-permute-start | bytes 688136 | tf_op jit(solution)/shard_map/ppermute | solution.py:20
  216.9 13.5 %collective-permute-done.41 = bf16[128,896]{1,0:T(8,128)(2,1)S(1)} collective-permute-done((bf16[128,896]{1,0:T(8,128)(2,1)S(1)}, bf16[128,896]{1,0:T(8,128)(2,1)S(1)}, u32[]{:S(2)}, u32[]{:S(2)}) %collective-permute-start.41) | collective-permute-done | bytes 229408 | tf_op jit(solution)/shard_map/ppermute | solution.py:20
  230.4 10.1 %collective-permute-done.39 = bf16[128,896]{1,0:T(8,128)(2,1)S(1)} collective-permute-done((bf16[128,896]{1,0:T(8,128)(2,1)S(1)}, bf16[128,896]{1,0:T(8,128)(2,1)S(1)}, u32[]{:S(2)}, u32[]{:S(2)}) %collective-permute-start.39) | collective-permute-done | bytes 229408 | tf_op jit(solution)/shard_map/ppermute | solution.py:20
  (88 shorter events, 71.3 us)
Async XLA Ops:
  31.6 36.0 %collective-permute-start.4 = (bf16[192,896]{1,0:T(8,128)(2,1)S(1)}, bf16[192,896]{1,0:T(8,128)(2,1)S(1)}, u32[]{:S(2)}, u32[]{:S(2)}) collective-permute-start(bf16[192,896]{1,0:T(8,128)(2,1)S(1)} %get-tuple-element.47), channel_id=1, source_target_pairs={{0,1},{1,2},{2,3},{3,0},{4,5},{5,6},{6,7},{7,4},{8,9},{9,10},{10,1... | collective-permute-start | bytes 1032200 | tf_op jit(solution)/shard_map/ppermute | solution.py:20
  32.1 35.6 %collective-permute-start.5 = (bf16[192,896]{1,0:T(8,128)(2,1)S(1)}, bf16[192,896]{1,0:T(8,128)(2,1)S(1)}, u32[]{:S(2)}, u32[]{:S(2)}) collective-permute-start(bf16[192,896]{1,0:T(8,128)(2,1)S(1)} %get-tuple-element.48), channel_id=1, source_target_pairs={{0,2},{1,3},{2,0},{3,1},{4,6},{5,7},{6,4},{7,5},{8,10},{9,11},{10,... | collective-permute-start | bytes 1032200 | tf_op jit(solution)/shard_map/ppermute | solution.py:20
  34.6 33.2 %collective-permute-start.6 = (bf16[192,896]{1,0:T(8,128)(2,1)S(1)}, bf16[192,896]{1,0:T(8,128)(2,1)S(1)}, u32[]{:S(2)}, u32[]{:S(2)}) collective-permute-start(bf16[192,896]{1,0:T(8,128)(2,1)S(1)} %get-tuple-element.49), channel_id=1, source_target_pairs={{0,3},{1,0},{2,1},{3,2},{4,7},{5,4},{6,5},{7,6},{8,11},{9,8},{10,9... | collective-permute-start | bytes 1032200 | tf_op jit(solution)/shard_map/ppermute | solution.py:20
  34.6 22.6 %collective-permute-start.23 = (bf16[144,896]{1,0:T(8,128)(2,1)S(1)}, bf16[144,896]{1,0:T(8,128)(2,1)S(1)}, u32[]{:S(2)}, u32[]{:S(2)}) collective-permute-start(bf16[144,896]{1,0:T(8,128)(2,1)S(1)} %pad_maximum_fusion.2.refs_0_), channel_id=1, source_target_pairs={{0,12},{1,13},{2,14},{3,15},{4,16},{5,17},{6,18},{7,19},{8,20},{9,... | collective-permute-start | bytes 774152 | tf_op jit(solution)/shard_map/ppermute | solution.py:20
  36.0 26.9 %collective-permute-start.24 = (bf16[144,896]{1,0:T(8,128)(2,1)S(1)}, bf16[144,896]{1,0:T(8,128)(2,1)S(1)}, u32[]{:S(2)}, u32[]{:S(2)}) collective-permute-start(bf16[144,896]{1,0:T(8,128)(2,1)S(1)} %pad_maximum_fusion.2.refs_0_), channel_id=1, source_target_pairs={{0,20},{1,21},{2,22},{3,23},{4,24},{5,25},{6,26},{7,27},{8,28},{9,... | collective-permute-start | bytes 774152 | tf_op jit(solution)/shard_map/ppermute | solution.py:20
  88.5 25.4 %collective-permute-start.28 = (bf16[4,2,96,1024]{3,2,1,0:T(8,128)(2,1)S(1)}, bf16[4,2,96,1024]{3,2,1,0:T(8,128)(2,1)S(1)}, u32[]{:S(2)}, u32[]{:S(2)}) collective-permute-start(bf16[4,2,96,1024]{3,2,1,0:T(8,128)(2,1)S(1)} %get-tuple-element.72), channel_id=1, source_target_pairs={{0,32},{32,0},{64,96},{96,64},{128,160},{160,128},{192,224},{224,1... | collective-permute-start | bytes 4718600 | tf_op jit(solution)/shard_map/ppermute | solution.py:29
  90.7 20.8 %collective-permute-start.9 = (bf16[2,96,1024]{2,1,0:T(8,128)(2,1)S(1)}, bf16[2,96,1024]{2,1,0:T(8,128)(2,1)S(1)}, u32[]{:S(2)}, u32[]{:S(2)}) collective-permute-start(bf16[2,96,1024]{2,1,0:T(8,128)(2,1)S(1)} %get-tuple-element.54), channel_id=1, source_target_pairs={{0,128},{32,160},{64,192},{96,224},{128,0},{160,32},{192,64},{224,... | collective-permute-start | bytes 1179656 | tf_op jit(solution)/shard_map/ppermute | solution.py:29
  93.6 17.9 %collective-permute-start.10 = (bf16[2,96,1024]{2,1,0:T(8,128)(2,1)S(1)}, bf16[2,96,1024]{2,1,0:T(8,128)(2,1)S(1)}, u32[]{:S(2)}, u32[]{:S(2)}) collective-permute-start(bf16[2,96,1024]{2,1,0:T(8,128)(2,1)S(1)} %get-tuple-element.55), channel_id=1, source_target_pairs={{0,192},{32,224},{64,0},{96,32},{128,64},{160,96},{192,128},{224,1... | collective-permute-start | bytes 1179656 | tf_op jit(solution)/shard_map/ppermute | solution.py:29
  114.3 29.1 %collective-permute-start.29 = (bf16[2,96,1024]{2,1,0:T(8,128)(2,1)S(1)}, bf16[2,96,1024]{2,1,0:T(8,128)(2,1)S(1)}, u32[]{:S(2)}, u32[]{:S(2)}) collective-permute-start(bf16[2,96,1024]{2,1,0:T(8,128)(2,1)S(1)} %get-tuple-element.74), channel_id=1, source_target_pairs={{0,64},{32,96},{64,128},{96,160},{128,192},{160,224},{192,0},{224,... | collective-permute-start | bytes 1179656 | tf_op jit(solution)/shard_map/ppermute | solution.py:29
  114.4 29.0 %collective-permute-start.30 = (bf16[2,96,1024]{2,1,0:T(8,128)(2,1)S(1)}, bf16[2,96,1024]{2,1,0:T(8,128)(2,1)S(1)}, u32[]{:S(2)}, u32[]{:S(2)}) collective-permute-start(bf16[2,96,1024]{2,1,0:T(8,128)(2,1)S(1)} %get-tuple-element.75), channel_id=1, source_target_pairs={{0,128},{32,160},{64,192},{96,224},{128,0},{160,32},{192,64},{224,... | collective-permute-start | bytes 1179656 | tf_op jit(solution)/shard_map/ppermute | solution.py:29
  116.8 26.6 %collective-permute-start.31 = (bf16[2,96,1024]{2,1,0:T(8,128)(2,1)S(1)}, bf16[2,96,1024]{2,1,0:T(8,128)(2,1)S(1)}, u32[]{:S(2)}, u32[]{:S(2)}) collective-permute-start(bf16[2,96,1024]{2,1,0:T(8,128)(2,1)S(1)} %get-tuple-element.76), channel_id=1, source_target_pairs={{0,192},{32,224},{64,0},{96,32},{128,64},{160,96},{192,128},{224,1... | collective-permute-start | bytes 1179656 | tf_op jit(solution)/shard_map/ppermute | solution.py:29
  118.2 21.4 %collective-permute-start.12 = (bf16[96,1024]{1,0:T(8,128)(2,1)S(1)}, bf16[96,1024]{1,0:T(8,128)(2,1)S(1)}, u32[]{:S(2)}, u32[]{:S(2)}) collective-permute-start(bf16[96,1024]{1,0:T(8,128)(2,1)S(1)} %shard_map.67), channel_id=1, source_target_pairs={{0,128},{32,160},{64,192},{96,224},{128,0},{160,32},{192,64},{224,... | collective-permute-start | bytes 589832 | tf_op jit(solution)/shard_map/ppermute | solution.py:29
  143.3 23.8 %collective-permute-start.14 = (bf16[4,96,1024]{2,1,0:T(8,128)(2,1)S(1)}, bf16[4,96,1024]{2,1,0:T(8,128)(2,1)S(1)}, u32[]{:S(2)}, u32[]{:S(2)}) collective-permute-start(bf16[4,96,1024]{2,1,0:T(8,128)(2,1)S(1)} %pad_maximum_fusion.refs_0_), channel_id=1, source_target_pairs={{0,32},{32,0},{64,96},{96,64},{128,160},{160,128},{192,224},{224,1... | collective-permute-start | bytes 2359304 | tf_op jit(solution)/shard_map/ppermute | solution.py:29
  143.7 17.8 %collective-permute-start.34 = (bf16[96,1024]{1,0:T(8,128)(2,1)S(1)}, bf16[96,1024]{1,0:T(8,128)(2,1)S(1)}, u32[]{:S(2)}, u32[]{:S(2)}) collective-permute-start(bf16[96,1024]{1,0:T(8,128)(2,1)S(1)} %shard_map.73), channel_id=1, source_target_pairs={{0,192},{32,224},{64,0},{96,32},{128,64},{160,96},{192,128},{224,1... | collective-permute-start | bytes 589832 | tf_op jit(solution)/shard_map/ppermute | solution.py:29
  169.8 19.5 %collective-permute-start.15 = (bf16[192,896]{1,0:T(8,128)(2,1)S(1)}, bf16[192,896]{1,0:T(8,128)(2,1)S(1)}, u32[]{:S(2)}, u32[]{:S(2)}) collective-permute-start(bf16[192,896]{1,0:T(8,128)(2,1)S(1)} %get-tuple-element.57), channel_id=1, source_target_pairs={{0,3},{1,0},{2,1},{3,2},{4,7},{5,4},{6,5},{7,6},{8,11},{9,8},{10,9... | collective-permute-start | bytes 1032200 | tf_op jit(solution)/shard_map/ppermute | solution.py:20
  171.0 18.4 %collective-permute-start.16 = (bf16[192,896]{1,0:T(8,128)(2,1)S(1)}, bf16[192,896]{1,0:T(8,128)(2,1)S(1)}, u32[]{:S(2)}, u32[]{:S(2)}) collective-permute-start(bf16[192,896]{1,0:T(8,128)(2,1)S(1)} %get-tuple-element.58), channel_id=1, source_target_pairs={{0,2},{1,3},{2,0},{3,1},{4,6},{5,7},{6,4},{7,5},{8,10},{9,11},{10,... | collective-permute-start | bytes 1032200 | tf_op jit(solution)/shard_map/ppermute | solution.py:20
  172.5 17.9 %collective-permute-start.17 = (bf16[192,896]{1,0:T(8,128)(2,1)S(1)}, bf16[192,896]{1,0:T(8,128)(2,1)S(1)}, u32[]{:S(2)}, u32[]{:S(2)}) collective-permute-start(bf16[192,896]{1,0:T(8,128)(2,1)S(1)} %get-tuple-element.59), channel_id=1, source_target_pairs={{0,1},{1,2},{2,3},{3,0},{4,5},{5,6},{6,7},{7,4},{8,9},{9,10},{10,1... | collective-permute-start | bytes 1032200 | tf_op jit(solution)/shard_map/ppermute | solution.py:20
  177.2 26.5 %collective-permute-start.36 = (bf16[192,896]{1,0:T(8,128)(2,1)S(1)}, bf16[192,896]{1,0:T(8,128)(2,1)S(1)}, u32[]{:S(2)}, u32[]{:S(2)}) collective-permute-start(bf16[192,896]{1,0:T(8,128)(2,1)S(1)} %get-tuple-element.78), channel_id=1, source_target_pairs={{0,3},{1,0},{2,1},{3,2},{4,7},{5,4},{6,5},{7,6},{8,11},{9,8},{10,9... | collective-permute-start | bytes 1032200 | tf_op jit(solution)/shard_map/ppermute | solution.py:20
  177.3 28.9 %collective-permute-start.37 = (bf16[192,896]{1,0:T(8,128)(2,1)S(1)}, bf16[192,896]{1,0:T(8,128)(2,1)S(1)}, u32[]{:S(2)}, u32[]{:S(2)}) collective-permute-start(bf16[192,896]{1,0:T(8,128)(2,1)S(1)} %get-tuple-element.79), channel_id=1, source_target_pairs={{0,2},{1,3},{2,0},{3,1},{4,6},{5,7},{6,4},{7,5},{8,10},{9,11},{10,... | collective-permute-start | bytes 1032200 | tf_op jit(solution)/shard_map/ppermute | solution.py:20
  191.3 17.7 %collective-permute-start.21 = (bf16[128,896]{1,0:T(8,128)(2,1)S(1)}, bf16[128,896]{1,0:T(8,128)(2,1)S(1)}, u32[]{:S(2)}, u32[]{:S(2)}) collective-permute-start(bf16[128,896]{1,0:T(8,128)(2,1)S(1)} %get-tuple-element.65), channel_id=1, source_target_pairs={{0,8},{1,9},{2,10},{3,11},{4,12},{5,13},{6,14},{7,15},{8,16},{9,17... | collective-permute-start | bytes 688136 | tf_op jit(solution)/shard_map/ppermute | solution.py:20
  194.1 18.9 %collective-permute-start.20 = (bf16[128,896]{1,0:T(8,128)(2,1)S(1)}, bf16[128,896]{1,0:T(8,128)(2,1)S(1)}, u32[]{:S(2)}, u32[]{:S(2)}) collective-permute-start(bf16[128,896]{1,0:T(8,128)(2,1)S(1)} %get-tuple-element.64), channel_id=1, source_target_pairs={{0,24},{1,25},{2,26},{3,27},{4,28},{5,29},{6,30},{7,31},{8,0},{9,1... | collective-permute-start | bytes 688136 | tf_op jit(solution)/shard_map/ppermute | solution.py:20
  208.0 22.5 %collective-permute-start.41 = (bf16[128,896]{1,0:T(8,128)(2,1)S(1)}, bf16[128,896]{1,0:T(8,128)(2,1)S(1)}, u32[]{:S(2)}, u32[]{:S(2)}) collective-permute-start(bf16[128,896]{1,0:T(8,128)(2,1)S(1)} %get-tuple-element.86), channel_id=1, source_target_pairs={{0,12},{1,13},{2,14},{3,15},{4,16},{5,17},{6,18},{7,19},{8,20},{9,... | collective-permute-start | bytes 688136 | tf_op jit(solution)/shard_map/ppermute | solution.py:20
  209.0 21.4 %collective-permute-start.40 = (bf16[128,896]{1,0:T(8,128)(2,1)S(1)}, bf16[128,896]{1,0:T(8,128)(2,1)S(1)}, u32[]{:S(2)}, u32[]{:S(2)}) collective-permute-start(bf16[128,896]{1,0:T(8,128)(2,1)S(1)} %get-tuple-element.85), channel_id=1, source_target_pairs={{0,20},{1,21},{2,22},{3,23},{4,24},{5,25},{6,26},{7,27},{8,28},{9,... | collective-permute-start | bytes 688136 | tf_op jit(solution)/shard_map/ppermute | solution.py:20
  213.1 27.4 %collective-permute-start.39 = (bf16[128,896]{1,0:T(8,128)(2,1)S(1)}, bf16[128,896]{1,0:T(8,128)(2,1)S(1)}, u32[]{:S(2)}, u32[]{:S(2)}) collective-permute-start(bf16[128,896]{1,0:T(8,128)(2,1)S(1)} %get-tuple-element.84), channel_id=1, source_target_pairs={{0,16},{1,17},{2,18},{3,19},{4,20},{5,21},{6,22},{7,23},{8,24},{9,... | collective-permute-start | bytes 688136 | tf_op jit(solution)/shard_map/ppermute | solution.py:20
  (22 other events, 314.1 us)
where the time goes:
time: 245 us; the launch traced here: 242 us
  waiting for transfers between devices  129 us (53%)
  starting transfers between devices  82.7 us (34%)
  Pallas kernels  23.7 us (10%)
  other arithmetic  3.55 us (1%)
    ppermute x26, waiting for transfers between devices, along_expert(): lax.ppermute(value, 'expert', [(i, (i // NX + dz) % planes * NX + (i % NX...  78.9 us
    ppermute x26, starting transfers between devices, along_expert(): lax.ppermute(value, 'expert', [(i, (i // NX + dz) % planes * NX + (i % NX...  55.8 us
    ppermute x16, waiting for transfers between devices, along_section(): lax.ppermute(value, 'section', [(i, (i + CORES * dy) % count ^ flip) for...  50.3 us
    ppermute x16, starting transfers between devices, along_section(): lax.ppermute(value, 'section', [(i, (i + CORES * dy) % count ^ flip) for...  26.9 us
    pallas_call x2, Pallas kernels, body(): call(functools.partial(up_kernel, held), [shape(4, 2, held, units)] * 2,...  11.8 us
    pallas_call x2, Pallas kernels, body(): call(functools.partial(down_kernel, held), [shape(2 * held, width)] * 4,...  5.35 us
  transfers between devices with their start and end apart: 42, of which 22 were waited for; matrix products, arithmetic and copies ran while one was open for 0% of the time, Pallas kernels for 10%

commit v1 on v0

v1 whole, which is shorter than its diff:
```python
import functools

import jax
import jax.numpy as jnp
from jax import lax
from jax.experimental import pallas as pl
from jax.experimental.pallas import tpu as pltpu
from jax.sharding import PartitionSpec as P

BF16, F32 = jnp.bfloat16, jnp.float32
NX, CORES = 4, 2
CHUNKS = ((1, -1), (2, -2), (3, -3), (0, 4))
VMEM = pl.BlockSpec(memory_space=pltpu.VMEM)
SMEM = pl.BlockSpec(memory_space=pltpu.SMEM)


def along_expert(value, dz, dx):
    count = lax.axis_size("expert")
    planes = count // NX
    return lax.ppermute(
        value,
        "expert",
        [(i, (i // NX + dz) % planes * NX + (i % NX + dx) % NX) for i in range(count)],
    )


def along_section(value, dy, flip):
    count = lax.axis_size("section")
    return lax.ppermute(
        value, "section", [(i, (i + CORES * dy) % count ^ flip) for i in range(count)]
    )


def call(kernel, outs, specs=None, grid=(), out_specs=None, scratch=(), limit=16, flops=0, moved=0):
    return pl.pallas_call(
        kernel,
        grid=grid,
        out_shape=outs,
        in_specs=specs,
        out_specs=out_specs or jax.tree.map(lambda _: VMEM, outs),
        scratch_shapes=scratch,
        compiler_params=pltpu.CompilerParams(vmem_limit_bytes=limit << 20),
        cost_estimate=pl.CostEstimate(flops=flops, bytes_accessed=moved, transcendentals=0),
    )


def select_kernel(capacity, rows, at_ref, *refs):
    nz = len(refs) - 3
    blocks, (out_ref, code_ref, weight_ref) = refs[:nz], refs[nz:]
    per_plane = 2 * NX
    row = lax.broadcasted_iota(jnp.int32, (per_plane, rows), 0)
    expert = (at_ref[0] * per_plane + row).astype(F32)
    earlier = (
        lax.broadcasted_iota(jnp.int32, (rows, rows), 0)
        < lax.broadcasted_iota(jnp.int32, (rows, rows), 1)
    ).astype(F32).astype(BF16)
    codes = []
    for n, block in enumerate(blocks):
        info = block[pl.ds(rows, 16), pl.ds(0, rows)].astype(F32)
        named = jnp.zeros((per_plane, rows), F32)
        weight = jnp.zeros((per_plane, rows), F32)
        for k in range(8):
            hit = info[k : k + 1] == expert
            named = named + jnp.where(hit, 1.0, 0.0)
            weight = weight + jnp.where(hit, info[8 + k : 9 + k], 0.0)
        slot = jnp.dot(named.astype(BF16), earlier, preferred_element_type=F32)
        codes.append(jnp.where(named > 0.5, slot + float(n * capacity), -1.0))
        weight_ref[:, pl.ds(n * rows, rows)] = weight
    code = jnp.concatenate(codes, axis=1)
    code_ref[...] = code
    held = nz * capacity
    at = lax.broadcasted_iota(jnp.int32, (held, nz * rows), 0).astype(F32)
    tokens = jnp.concatenate([block[pl.ds(0, rows), :] for block in blocks], axis=0)
    for r in range(NX):
        pick = jnp.concatenate(
            [jnp.where(at == code[2 * r + e : 2 * r + e + 1], 1.0, 0.0) for e in range(2)], axis=0
        ).astype(BF16)
        out_ref[r] = jnp.dot(pick, tokens, preferred_element_type=F32).astype(BF16)


def up_kernel(held, at_ref, rows_ref, gate_ref, up_ref, keep_ref, send_ref, x_ref):
    core = at_ref[1]

    @pl.when(pl.program_id(0) == 0)
    def _():
        for r in range(4):
            for e in range(2):
                x_ref[e, pl.ds(r * held, held), :] = rows_ref[r, pl.ds(e * held, held), :]

    for out_ref, e in ((keep_ref, core), (send_ref, 1 - core)):
        x = x_ref[e]
        for part, weight_ref in enumerate((gate_ref, up_ref)):
            sums = jnp.dot(x, weight_ref[e], preferred_element_type=F32).astype(BF16)
            for r in range(4):
                out_ref[r, part] = sums[r * held : (r + 1) * held]


def join_kernel(keep_ref, got_ref, out_ref):
    out_ref[...] = (keep_ref[...].astype(F32) + got_ref[...].astype(F32)).astype(BF16)


def silu_kernel(terms_ref, out_ref):
    gate, up = (
        (terms_ref[0, i].astype(F32) + terms_ref[1, i].astype(F32))
        + (terms_ref[2, i].astype(F32) + terms_ref[3, i].astype(F32))
        for i in range(2)
    )
    hidden = (jax.nn.silu(gate) * up).astype(BF16)
    for q in range(4):
        out_ref[q] = hidden


def down_kernel(held, at_ref, own_ref, other_ref, down_ref, out_ref):
    core = at_ref[1]
    for parts_ref, e in ((own_ref, core), (other_ref, 1 - core)):
        hidden = parts_ref[...].reshape(4 * held, parts_ref.shape[2])
        got = jnp.dot(hidden, down_ref[e], preferred_element_type=F32).astype(BF16)
        for r in range(4):
            out_ref[r, e] = got[r * held : (r + 1) * held]


def mix_kernel(held, rows, back_ref, code_ref, weight_ref, *outs):
    width = code_ref.shape[1]
    at = lax.broadcasted_iota(jnp.int32, (held, width), 0).astype(F32)
    share = jnp.concatenate(
        [
            jnp.where(at == code_ref[j : j + 1, :], weight_ref[j : j + 1, :], 0.0)
            for j in range(2 * NX)
        ],
        axis=0,
    ).astype(BF16)
    total = lax.dot_general(
        share,
        back_ref[...].reshape(share.shape[0], back_ref.shape[3]),
        (((0,), (0,)), ((), ())),
        preferred_element_type=F32,
    ).astype(BF16)
    for n, out in enumerate(outs):
        out[...] = total[n * rows : (n + 1) * rows]


def shape(*dims, dtype=BF16):
    return jax.ShapeDtypeStruct(dims, dtype)


def body(tokens, routes, combine, gate_weight, up_weight, down_weight):
    groups = lax.axis_size("expert")
    per_device, width, units = gate_weight.shape
    rows, fanout = routes.shape
    capacity = 3 * rows * fanout // (2 * per_device * groups)
    place, part = lax.axis_index("expert"), lax.axis_index("section")
    at = jnp.stack([place // NX, part % CORES]).astype(jnp.int32)
    planes = groups // NX
    x_groups = [[z * NX + x for x in range(NX)] for z in range(planes)]
    sections = lax.axis_size("section")
    y_groups = [[y * CORES + c for y in range(sections // CORES)] for c in range(CORES)]

    def swap_x(value):
        return lax.all_to_all(value, "expert", 0, 0, axis_index_groups=x_groups, tiled=True)

    def swap_y(value):
        return lax.all_to_all(value, "section", 0, 0, axis_index_groups=y_groups, tiled=True)

    info = jnp.concatenate([routes.T.astype(BF16), combine.T.astype(BF16)], axis=0)
    block = {0: jnp.concatenate([tokens, jnp.pad(info, ((0, 0), (0, width - rows)))], axis=0)}
    for d in (1, -1, 2, -2, 3, -3, 4):
        step = 1 if d > 0 else -1
        block[d] = along_expert(block[d - step], step, 0)

    partials = []
    for chunk in CHUNKS:
        nz = len(chunk)
        held = nz * capacity
        picked, code, weight = call(
            functools.partial(select_kernel, capacity, rows),
            [shape(4, 2 * held, width)] + [shape(2 * NX, nz * rows, dtype=F32)] * 2,
            [SMEM] + [VMEM] * nz,
            flops=16 * held * nz * rows * width,
            moved=2 << 20,
        )(at, *[block[d] for d in chunk])
        came = swap_x(picked)
        tile = 256
        keep, send = call(
            functools.partial(up_kernel, held),
            [shape(4, 2, held, units)] * 2,
            [SMEM, pl.BlockSpec((4, 2 * held, width), lambda i: (0, 0, 0))]
            + [pl.BlockSpec((2, width, tile), lambda i: (0, 0, i))] * 2,
            grid=(units // tile,),
            out_specs=[pl.BlockSpec((4, 2, held, tile), lambda i: (0, 0, 0, i))] * 2,
            scratch=[pltpu.VMEM((2, 4 * held, width), BF16)],
            flops=32 * held * width * units,
            moved=10 << 20,
        )(at, came, gate_weight, up_weight)
        got = along_section(send, 0, 1)
        sums = call(join_kernel, shape(4, 2, held, units), [VMEM] * 2, moved=3 << 20)(keep, got)
        terms = swap_y(sums)
        hidden = call(silu_kernel, shape(4, held, units), [VMEM], moved=1 << 20)(terms)
        parts = swap_y(hidden)
        others = along_section(parts, 0, 1)
        out = call(
            functools.partial(down_kernel, held),
            shape(4, 2, held, width),
            [SMEM, VMEM, VMEM, VMEM],
            flops=16 * held * width * units,
            moved=6 << 20,
        )(at, parts, others, down_weight)
        back = swap_x(out)
        mixed = call(
            functools.partial(mix_kernel, held, rows),
            [shape(rows, width)] * nz,
            [VMEM] * 3,
            flops=16 * held * nz * rows * width,
            moved=2 << 20,
        )(back, code, weight)
        partials += [along_expert(m, -d, 0) if d else m for d, m in zip(chunk, mixed)]
    return sum(p.astype(F32) for p in partials).astype(BF16)


def solution(mesh):
    return jax.shard_map(
        body,
        mesh=mesh,
        in_specs=(
            P("expert", "section"),
            P("expert", None),
            P("expert", None),
            P("expert", "section", None),
            P("expert", "section", None),
            P("expert", None, "section"),
        ),
        out_specs=P("expert", "section"),
        check_vma=False,
    )
```

time: 245 us -> 279 us (1.14)
  the two profiles are of different devices: /device:TPU:6 before, /device:TPU:66 now
where the time goes in v1:
time: 279 us; the launch traced here: 277 us
  waiting for transfers between devices  104 us (37%)
  starting transfers between devices  90.9 us (33%)
  Pallas kernels  49.7 us (18%)
  local copies, waits for them, and re-layouts  28.3 us (10%)
  other arithmetic  4.39 us (2%)
    ppermute x14, waiting for transfers between devices, along_expert(): lax.ppermute(value, 'expert', [(i, (i // NX + dz) % planes * NX + (i % NX...  47.7 us
    all_to_all x8, waiting for transfers between devices, swap_y(): lax.all_to_all(value, 'section', 0, 0, axis_index_groups=y_groups, tiled=...  45.7 us
    all_to_all x8, starting transfers between devices, swap_x(): lax.all_to_all(value, 'expert', 0, 0, axis_index_groups=x_groups, tiled=T...  38.8 us
    all_to_all x8, starting transfers between devices, swap_y(): lax.all_to_all(value, 'section', 0, 0, axis_index_groups=y_groups, tiled=...  28.8 us
    unnamed x36, local copies, waits for them, and re-layouts  28.3 us
    ppermute x14, starting transfers between devices, along_expert(): lax.ppermute(value, 'expert', [(i, (i // NX + dz) % planes * NX + (i % NX...  23.3 us
    pallas_call x4, Pallas kernels, body(): call(functools.partial(up_kernel, held), [shape(4, 2, held, units)] * 2,...  17.9 us
    pallas_call x4, Pallas kernels, body(): call(functools.partial(down_kernel, held), shape(4, 2, held, width), [SME...  9.7 us
  transfers between devices with their start and end apart: 38, of which 25 were waited for; matrix products, arithmetic and copies ran while one was open for 0% of the time, Pallas kernels for 17%

profile of v1, /device:TPU:66, one launch (start us, length us, event | category | flops | bytes accessed | tf_op | source)
XLA Modules:
  0.0 277.2 jit_solution(6183888577580363252)
XLA Ops:
  4.5 5.9 %collective-permute-done.refs_0_ = bf16[144,896]{1,0:T(8,128)(2,1)S(1)} collective-permute-done((bf16[144,896]{1,0:T(8,128)(2,1)S(1)}, bf16[144,896]{1,0:T(8,128)(2,1)S(1)}, u32[]{:S(2)}, u32[]{:S(2)}) %collective-permute-start) | collective-permute-done | bytes 258080 | tf_op jit(solution)/shard_map/ppermute | solution.py:20
  15.4 4.8 %all-to-all-start = ((bf16[4,96,896]{2,1,0:T(8,128)(2,1)}), bf16[4,96,896]{2,1,0:T(8,128)(2,1)S(1)}, u32[]{:S(2)}, u32[]{:S(2)}) async-start(bf16[4,96,896]{2,1,0:T(8,128)(2,1)} %get-tuple-element.33), calls=%async_computation | async-start | bytes 1376256 | tf_op jit(solution)/shard_map/all_to_all | solution.py:159
  23.1 3.8 %collective-permute-done.6.refs_0_ = bf16[144,896]{1,0:T(8,128)(2,1)S(1)} collective-permute-done((bf16[144,896]{1,0:T(8,128)(2,1)S(1)}, bf16[144,896]{1,0:T(8,128)(2,1)S(1)}, u32[]{:S(2)}, u32[]{:S(2)}) %collective-permute-start.6) | collective-permute-done | bytes 258080 | tf_op jit(solution)/shard_map/ppermute | solution.py:20
  31.5 4.8 %all-to-all-start.4 = ((bf16[4,96,896]{2,1,0:T(8,128)(2,1)}), bf16[4,96,896]{2,1,0:T(8,128)(2,1)S(1)}, u32[]{:S(2)}, u32[]{:S(2)}) async-start(bf16[4,96,896]{2,1,0:T(8,128)(2,1)} %get-tuple-element.40), calls=%async_computation.4 | async-start | bytes 1376256 | tf_op jit(solution)/shard_map/all_to_all | solution.py:159
  38.3 4.4 %collective-permute-done.12.refs_0_ = bf16[144,896]{1,0:T(8,128)(2,1)} collective-permute-done((bf16[144,896]{1,0:T(8,128)(2,1)S(1)}, bf16[144,896]{1,0:T(8,128)(2,1)}, u32[]{:S(2)}, u32[]{:S(2)}) %collective-permute-start.12) | collective-permute-done | bytes 258080 | tf_op jit(solution)/shard_map/ppermute | solution.py:20
  46.5 4.8 %all-to-all-start.8 = ((bf16[4,96,896]{2,1,0:T(8,128)(2,1)}), bf16[4,96,896]{2,1,0:T(8,128)(2,1)S(1)}, u32[]{:S(2)}, u32[]{:S(2)}) async-start(bf16[4,96,896]{2,1,0:T(8,128)(2,1)} %get-tuple-element.47), calls=%async_computation.8 | async-start | bytes 1376256 | tf_op jit(solution)/shard_map/all_to_all | solution.py:159
  56.7 4.5 %shard_map.65 = (bf16[4,2,48,1024]{3,2,1,0:T(8,128)(2,1)S(1)}, bf16[4,2,48,1024]{3,2,1,0:T(8,128)(2,1)}) custom-call(s32[2]{0:T(128)S(1)} %pad_add_fusion.at_ref, bf16[4,96,896]{2,1,0:T(8,128)(2,1)S(1)} %all-to-all-done.rows_ref, bf16[2,896,1024]{2,1,0:T(8,128)(2,1)S(1)} %copy-done, bf16[2,896,1024]{2,1,0:T(8,128)(2,1)S(1)} %copy-done.4), custom_call_target="tpu_custom_call" | custom-call | flops 1409286144 | bytes 10485760 | tf_op jit(solution)/shard_map/pallas_call | solution.py:183
  64.1 4.8 %all-to-all-start.12 = ((bf16[4,96,896]{2,1,0:T(8,128)(2,1)}), bf16[4,96,896]{2,1,0:T(8,128)(2,1)S(1)}, u32[]{:S(2)}, u32[]{:S(2)}) async-start(bf16[4,96,896]{2,1,0:T(8,128)(2,1)} %get-tuple-element.54), calls=%async_computation.12 | async-start | bytes 1376256 | tf_op jit(solution)/shard_map/all_to_all | solution.py:159
  72.9 4.5 %shard_map.71 = (bf16[4,2,48,1024]{3,2,1,0:T(8,128)(2,1)S(1)}, bf16[4,2,48,1024]{3,2,1,0:T(8,128)(2,1)}) custom-call(s32[2]{0:T(128)S(1)} %pad_add_fusion.at_ref, bf16[4,96,896]{2,1,0:T(8,128)(2,1)S(1)} %all-to-all-done.4.rows_ref, bf16[2,896,1024]{2,1,0:T(8,128)(2,1)S(1)} %copy-done.1, bf16[2,896,1024]{2,1,0:T(8,128)(2,1)S(1)} %copy-done.5), custom_call_target="tpu_custom_call" | custom-call | flops 1409286144 | bytes 10485760 | tf_op jit(solution)/shard_map/pallas_call | solution.py:183
  80.6 4.5 %all-to-all-start.1 = ((bf16[4,2,48,1024]{3,2,1,0:T(8,128)(2,1)}), bf16[4,2,48,1024]{3,2,1,0:T(8,128)(2,1)S(1)}, u32[]{:S(2)}, u32[]{:S(2)}) async-start(bf16[4,2,48,1024]{3,2,1,0:T(8,128)(2,1)} %shard_map.66), calls=%async_computation.1 | async-start | bytes 1572864 | tf_op jit(solution)/shard_map/all_to_all | solution.py:162
  87.3 10.7 %all-to-all-done.1.terms_ref = bf16[4,2,48,1024]{3,2,1,0:T(8,128)(2,1)S(1)} async-done(((bf16[4,2,48,1024]{3,2,1,0:T(8,128)(2,1)}), bf16[4,2,48,1024]{3,2,1,0:T(8,128)(2,1)S(1)}, u32[]{:S(2)}, u32[]{:S(2)}) %all-to-all-start.1) | async-done | bytes 786464 | tf_op jit(solution)/shard_map/all_to_all | solution.py:162
  105.6 4.5 %shard_map.77 = (bf16[4,2,48,1024]{3,2,1,0:T(8,128)(2,1)S(1)}, bf16[4,2,48,1024]{3,2,1,0:T(8,128)(2,1)}) custom-call(s32[2]{0:T(128)S(1)} %pad_add_fusion.at_ref, bf16[4,96,896]{2,1,0:T(8,128)(2,1)S(1)} %all-to-all-done.8.rows_ref, bf16[2,896,1024]{2,1,0:T(8,128)(2,1)S(1)} %copy-done.2, bf16[2,896,1024]{2,1,0:T(8,128)(2,1)S(1)} %copy-done.6), custom_call_target="tpu_custom_call" | custom-call | flops 1409286144 | bytes 10485760 | tf_op jit(solution)/shard_map/pallas_call | solution.py:183
  119.2 6.1 %all-to-all-done.2.own_ref = bf16[4,48,1024]{2,1,0:T(8,128)(2,1)S(1)} async-done(((bf16[4,48,1024]{2,1,0:T(8,128)(2,1)}), bf16[4,48,1024]{2,1,0:T(8,128)(2,1)S(1)}, u32[]{:S(2)}, u32[]{:S(2)}) %all-to-all-start.2) | async-done | bytes 393248 | tf_op jit(solution)/shard_map/all_to_all | solution.py:162
  132.9 4.5 %shard_map.83 = (bf16[4,2,48,1024]{3,2,1,0:T(8,128)(2,1)S(1)}, bf16[4,2,48,1024]{3,2,1,0:T(8,128)(2,1)}) custom-call(s32[2]{0:T(128)S(1)} %pad_add_fusion.at_ref, bf16[4,96,896]{2,1,0:T(8,128)(2,1)S(1)} %all-to-all-done.12.rows_ref, bf16[2,896,1024]{2,1,0:T(8,128)(2,1)S(1)} %copy-done.3, bf16[2,896,1024]{2,1,0:T(8,128)(2,1)S(1)} %copy-done.7), custom_call_target="tpu_custom_call" | custom-call | flops 1409286144 | bytes 10485760 | tf_op jit(solution)/shard_map/pallas_call | solution.py:183
  145.9 5.8 %all-to-all-done.6.own_ref = bf16[4,48,1024]{2,1,0:T(8,128)(2,1)S(1)} async-done(((bf16[4,48,1024]{2,1,0:T(8,128)(2,1)}), bf16[4,48,1024]{2,1,0:T(8,128)(2,1)S(1)}, u32[]{:S(2)}, u32[]{:S(2)}) %all-to-all-start.6) | async-done | bytes 393248 | tf_op jit(solution)/shard_map/all_to_all | solution.py:162
  156.2 10.2 %all-to-all-done.13.terms_ref = bf16[4,2,48,1024]{3,2,1,0:T(8,128)(2,1)S(1)} async-done(((bf16[4,2,48,1024]{3,2,1,0:T(8,128)(2,1)}), bf16[4,2,48,1024]{3,2,1,0:T(8,128)(2,1)S(1)}, u32[]{:S(2)}, u32[]{:S(2)}) %all-to-all-start.13) | async-done | bytes 786464 | tf_op jit(solution)/shard_map/all_to_all | solution.py:162
  170.8 6.4 %all-to-all-done.10.own_ref = bf16[4,48,1024]{2,1,0:T(8,128)(2,1)S(1)} async-done(((bf16[4,48,1024]{2,1,0:T(8,128)(2,1)}), bf16[4,48,1024]{2,1,0:T(8,128)(2,1)S(1)}, u32[]{:S(2)}, u32[]{:S(2)}) %all-to-all-start.10) | async-done | bytes 393248 | tf_op jit(solution)/shard_map/all_to_all | solution.py:162
  188.0 4.8 %all-to-all-start.3 = ((bf16[4,2,48,896]{3,2,1,0:T(8,128)(2,1)}), bf16[4,2,48,896]{3,2,1,0:T(8,128)(2,1)S(1)}, u32[]{:S(2)}, u32[]{:S(2)}) async-start(bf16[4,2,48,896]{3,2,1,0:T(8,128)(2,1)} %shard_map.68), calls=%async_computation.3 | async-start | bytes 1376256 | tf_op jit(solution)/shard_map/all_to_all | solution.py:159
  200.3 4.9 %all-to-all-start.7 = ((bf16[4,2,48,896]{3,2,1,0:T(8,128)(2,1)}), bf16[4,2,48,896]{3,2,1,0:T(8,128)(2,1)S(1)}, u32[]{:S(2)}, u32[]{:S(2)}) async-start(bf16[4,2,48,896]{3,2,1,0:T(8,128)(2,1)} %shard_map.74), calls=%async_computation.7 | async-start | bytes 1376256 | tf_op jit(solution)/shard_map/all_to_all | solution.py:159
  213.9 4.9 %all-to-all-start.11 = ((bf16[4,2,48,896]{3,2,1,0:T(8,128)(2,1)}), bf16[4,2,48,896]{3,2,1,0:T(8,128)(2,1)S(1)}, u32[]{:S(2)}, u32[]{:S(2)}) async-start(bf16[4,2,48,896]{3,2,1,0:T(8,128)(2,1)} %shard_map.80), calls=%async_computation.11 | async-start | bytes 1376256 | tf_op jit(solution)/shard_map/all_to_all | solution.py:159
  226.3 4.9 %all-to-all-start.15 = ((bf16[4,2,48,896]{3,2,1,0:T(8,128)(2,1)}), bf16[4,2,48,896]{3,2,1,0:T(8,128)(2,1)S(1)}, u32[]{:S(2)}, u32[]{:S(2)}) async-start(bf16[4,2,48,896]{3,2,1,0:T(8,128)(2,1)} %shard_map.86), calls=%async_computation.15 | async-start | bytes 1376256 | tf_op jit(solution)/shard_map/all_to_all | solution.py:159
  250.8 8.6 %collective-permute-done.10 = bf16[128,896]{1,0:T(8,128)(2,1)S(1)} collective-permute-done((bf16[128,896]{1,0:T(8,128)(2,1)S(1)}, bf16[128,896]{1,0:T(8,128)(2,1)S(1)}, u32[]{:S(2)}, u32[]{:S(2)}) %collective-permute-start.10) | collective-permute-done | bytes 229408 | tf_op jit(solution)/shard_map/ppermute | solution.py:20
  259.4 8.9 %collective-permute-done.16 = bf16[128,896]{1,0:T(8,128)(2,1)S(1)} collective-permute-done((bf16[128,896]{1,0:T(8,128)(2,1)S(1)}, bf16[128,896]{1,0:T(8,128)(2,1)S(1)}, u32[]{:S(2)}, u32[]{:S(2)}) %collective-permute-start.16) | collective-permute-done | bytes 229408 | tf_op jit(solution)/shard_map/ppermute | solution.py:20
  268.3 7.0 %collective-permute-done.17 = bf16[128,896]{1,0:T(8,128)(2,1)S(1)} collective-permute-done((bf16[128,896]{1,0:T(8,128)(2,1)S(1)}, bf16[128,896]{1,0:T(8,128)(2,1)S(1)}, u32[]{:S(2)}, u32[]{:S(2)}) %collective-permute-start.17) | collective-permute-done | bytes 229408 | tf_op jit(solution)/shard_map/ppermute | solution.py:20
  (118 shorter events, 138.1 us)
Async XLA Ops:
  15.4 16.1 %all-to-all-start = ((bf16[4,96,896]{2,1,0:T(8,128)(2,1)}), bf16[4,96,896]{2,1,0:T(8,128)(2,1)S(1)}, u32[]{:S(2)}, u32[]{:S(2)}) async-start(bf16[4,96,896]{2,1,0:T(8,128)(2,1)} %get-tuple-element.33), calls=%async_computation | async-start | bytes 1376256 | tf_op jit(solution)/shard_map/all_to_all | solution.py:159
  31.5 15.0 %all-to-all-start.4 = ((bf16[4,96,896]{2,1,0:T(8,128)(2,1)}), bf16[4,96,896]{2,1,0:T(8,128)(2,1)S(1)}, u32[]{:S(2)}, u32[]{:S(2)}) async-start(bf16[4,96,896]{2,1,0:T(8,128)(2,1)} %get-tuple-element.40), calls=%async_computation.4 | async-start | bytes 1376256 | tf_op jit(solution)/shard_map/all_to_all | solution.py:159
  46.5 17.6 %all-to-all-start.8 = ((bf16[4,96,896]{2,1,0:T(8,128)(2,1)}), bf16[4,96,896]{2,1,0:T(8,128)(2,1)S(1)}, u32[]{:S(2)}, u32[]{:S(2)}) async-start(bf16[4,96,896]{2,1,0:T(8,128)(2,1)} %get-tuple-element.47), calls=%async_computation.8 | async-start | bytes 1376256 | tf_op jit(solution)/shard_map/all_to_all | solution.py:159
  51.3 10.8 %collective-permute-start.18 = (bf16[144,896]{1,0:T(8,128)(2,1)}, bf16[144,896]{1,0:T(8,128)(2,1)S(1)}, u32[]{:S(2)}, u32[]{:S(2)}) collective-permute-start(bf16[144,896]{1,0:T(8,128)(2,1)} %collective-permute-done.12.refs_0_), channel_id=1, source_target_pairs={{0,4},{1,5},{2,6},{3,7},{4,8},{5,9},{6,10},{7,11},{8,12},{9,13},{1... | collective-permute-start | bytes 774152 | tf_op jit(solution)/shard_map/ppermute | solution.py:20
  62.1 16.3 %collective-permute-start.2 = (bf16[4,2,48,1024]{3,2,1,0:T(8,128)(2,1)}, bf16[4,2,48,1024]{3,2,1,0:T(8,128)(2,1)}, u32[]{:S(2)}, u32[]{:S(2)}) collective-permute-start(bf16[4,2,48,1024]{3,2,1,0:T(8,128)(2,1)} %get-tuple-element.35), channel_id=1, source_target_pairs={{0,32},{32,0},{64,96},{96,64},{128,160},{160,128},{192,224},{224,1... | collective-permute-start | bytes 2359304 | tf_op jit(solution)/shard_map/ppermute | solution.py:29
  64.1 16.6 %all-to-all-start.12 = ((bf16[4,96,896]{2,1,0:T(8,128)(2,1)}), bf16[4,96,896]{2,1,0:T(8,128)(2,1)S(1)}, u32[]{:S(2)}, u32[]{:S(2)}) async-start(bf16[4,96,896]{2,1,0:T(8,128)(2,1)} %get-tuple-element.54), calls=%async_computation.12 | async-start | bytes 1376256 | tf_op jit(solution)/shard_map/all_to_all | solution.py:159
  80.6 17.4 %all-to-all-start.1 = ((bf16[4,2,48,1024]{3,2,1,0:T(8,128)(2,1)}), bf16[4,2,48,1024]{3,2,1,0:T(8,128)(2,1)S(1)}, u32[]{:S(2)}, u32[]{:S(2)}) async-start(bf16[4,2,48,1024]{3,2,1,0:T(8,128)(2,1)} %shard_map.66), calls=%async_computation.1 | async-start | bytes 1572864 | tf_op jit(solution)/shard_map/all_to_all | solution.py:162
  98.0 15.5 %all-to-all-start.5 = ((bf16[4,2,48,1024]{3,2,1,0:T(8,128)(2,1)}), bf16[4,2,48,1024]{3,2,1,0:T(8,128)(2,1)S(1)}, u32[]{:S(2)}, u32[]{:S(2)}) async-start(bf16[4,2,48,1024]{3,2,1,0:T(8,128)(2,1)} %shard_map.72), calls=%async_computation.5 | async-start | bytes 1572864 | tf_op jit(solution)/shard_map/all_to_all | solution.py:162
  113.5 11.8 %all-to-all-start.2 = ((bf16[4,48,1024]{2,1,0:T(8,128)(2,1)}), bf16[4,48,1024]{2,1,0:T(8,128)(2,1)S(1)}, u32[]{:S(2)}, u32[]{:S(2)}) async-start(bf16[4,48,1024]{2,1,0:T(8,128)(2,1)} %shard_map.67), calls=%async_computation.2 | async-start | bytes 786432 | tf_op jit(solution)/shard_map/all_to_all | solution.py:162
  125.4 14.9 %all-to-all-start.9 = ((bf16[4,2,48,1024]{3,2,1,0:T(8,128)(2,1)}), bf16[4,2,48,1024]{3,2,1,0:T(8,128)(2,1)S(1)}, u32[]{:S(2)}, u32[]{:S(2)}) async-start(bf16[4,2,48,1024]{3,2,1,0:T(8,128)(2,1)} %shard_map.78), calls=%async_computation.9 | async-start | bytes 1572864 | tf_op jit(solution)/shard_map/all_to_all | solution.py:162
  140.3 11.5 %all-to-all-start.6 = ((bf16[4,48,1024]{2,1,0:T(8,128)(2,1)}), bf16[4,48,1024]{2,1,0:T(8,128)(2,1)S(1)}, u32[]{:S(2)}, u32[]{:S(2)}) async-start(bf16[4,48,1024]{2,1,0:T(8,128)(2,1)} %shard_map.73), calls=%async_computation.6 | async-start | bytes 786432 | tf_op jit(solution)/shard_map/all_to_all | solution.py:162
  151.8 14.6 %all-to-all-start.13 = ((bf16[4,2,48,1024]{3,2,1,0:T(8,128)(2,1)}), bf16[4,2,48,1024]{3,2,1,0:T(8,128)(2,1)S(1)}, u32[]{:S(2)}, u32[]{:S(2)}) async-start(bf16[4,2,48,1024]{3,2,1,0:T(8,128)(2,1)} %shard_map.84), calls=%async_computation.13 | async-start | bytes 1572864 | tf_op jit(solution)/shard_map/all_to_all | solution.py:162
  166.4 10.8 %all-to-all-start.10 = ((bf16[4,48,1024]{2,1,0:T(8,128)(2,1)}), bf16[4,48,1024]{2,1,0:T(8,128)(2,1)S(1)}, u32[]{:S(2)}, u32[]{:S(2)}) async-start(bf16[4,48,1024]{2,1,0:T(8,128)(2,1)} %shard_map.79), calls=%async_computation.10 | async-start | bytes 786432 | tf_op jit(solution)/shard_map/all_to_all | solution.py:162
  169.8 10.8 %collective-permute-start.3 = (bf16[4,48,1024]{2,1,0:T(8,128)(2,1)S(1)}, bf16[4,48,1024]{2,1,0:T(8,128)(2,1)S(1)}, u32[]{:S(2)}, u32[]{:S(2)}) collective-permute-start(bf16[4,48,1024]{2,1,0:T(8,128)(2,1)S(1)} %all-to-all-done.2.own_ref), channel_id=1, source_target_pairs={{0,32},{32,0},{64,96},{96,64},{128,160},{160,128},{192,224},{224,1... | collective-permute-start | bytes 1179656 | tf_op jit(solution)/shard_map/ppermute | solution.py:29
  188.0 12.3 %all-to-all-start.3 = ((bf16[4,2,48,896]{3,2,1,0:T(8,128)(2,1)}), bf16[4,2,48,896]{3,2,1,0:T(8,128)(2,1)S(1)}, u32[]{:S(2)}, u32[]{:S(2)}) async-start(bf16[4,2,48,896]{3,2,1,0:T(8,128)(2,1)} %shard_map.68), calls=%async_computation.3 | async-start | bytes 1376256 | tf_op jit(solution)/shard_map/all_to_all | solution.py:159
  200.3 13.6 %all-to-all-start.7 = ((bf16[4,2,48,896]{3,2,1,0:T(8,128)(2,1)}), bf16[4,2,48,896]{3,2,1,0:T(8,128)(2,1)S(1)}, u32[]{:S(2)}, u32[]{:S(2)}) async-start(bf16[4,2,48,896]{3,2,1,0:T(8,128)(2,1)} %shard_map.74), calls=%async_computation.7 | async-start | bytes 1376256 | tf_op jit(solution)/shard_map/all_to_all | solution.py:159
  213.9 12.4 %all-to-all-start.11 = ((bf16[4,2,48,896]{3,2,1,0:T(8,128)(2,1)}), bf16[4,2,48,896]{3,2,1,0:T(8,128)(2,1)S(1)}, u32[]{:S(2)}, u32[]{:S(2)}) async-start(bf16[4,2,48,896]{3,2,1,0:T(8,128)(2,1)} %shard_map.80), calls=%async_computation.11 | async-start | bytes 1376256 | tf_op jit(solution)/shard_map/all_to_all | solution.py:159
  226.3 15.8 %all-to-all-start.15 = ((bf16[4,2,48,896]{3,2,1,0:T(8,128)(2,1)}), bf16[4,2,48,896]{3,2,1,0:T(8,128)(2,1)S(1)}, u32[]{:S(2)}, u32[]{:S(2)}) async-start(bf16[4,2,48,896]{3,2,1,0:T(8,128)(2,1)} %shard_map.86), calls=%async_computation.15 | async-start | bytes 1376256 | tf_op jit(solution)/shard_map/all_to_all | solution.py:159
  233.0 14.0 %collective-permute-start.5 = (bf16[128,896]{1,0:T(8,128)(2,1)S(1)}, bf16[128,896]{1,0:T(8,128)(2,1)}, u32[]{:S(2)}, u32[]{:S(2)}) collective-permute-start(bf16[128,896]{1,0:T(8,128)(2,1)S(1)} %get-tuple-element.39), channel_id=1, source_target_pairs={{0,4},{1,5},{2,6},{3,7},{4,8},{5,9},{6,10},{7,11},{8,12},{9,13},{1... | collective-permute-start | bytes 688136 | tf_op jit(solution)/shard_map/ppermute | solution.py:20
  234.8 24.5 %collective-permute-start.10 = (bf16[128,896]{1,0:T(8,128)(2,1)S(1)}, bf16[128,896]{1,0:T(8,128)(2,1)S(1)}, u32[]{:S(2)}, u32[]{:S(2)}) collective-permute-start(bf16[128,896]{1,0:T(8,128)(2,1)S(1)} %get-tuple-element.45), channel_id=1, source_target_pairs={{0,24},{1,25},{2,26},{3,27},{4,28},{5,29},{6,30},{7,31},{8,0},{9,1... | collective-permute-start | bytes 688136 | tf_op jit(solution)/shard_map/ppermute | solution.py:20
  235.5 23.9 %collective-permute-start.11 = (bf16[128,896]{1,0:T(8,128)(2,1)S(1)}, bf16[128,896]{1,0:T(8,128)(2,1)S(1)}, u32[]{:S(2)}, u32[]{:S(2)}) collective-permute-start(bf16[128,896]{1,0:T(8,128)(2,1)S(1)} %get-tuple-element.46), channel_id=1, source_target_pairs={{0,8},{1,9},{2,10},{3,11},{4,12},{5,13},{6,14},{7,15},{8,16},{9,17... | collective-permute-start | bytes 688136 | tf_op jit(solution)/shard_map/ppermute | solution.py:20
  239.5 28.8 %collective-permute-start.16 = (bf16[128,896]{1,0:T(8,128)(2,1)S(1)}, bf16[128,896]{1,0:T(8,128)(2,1)S(1)}, u32[]{:S(2)}, u32[]{:S(2)}) collective-permute-start(bf16[128,896]{1,0:T(8,128)(2,1)S(1)} %get-tuple-element.52), channel_id=1, source_target_pairs={{0,20},{1,21},{2,22},{3,23},{4,24},{5,25},{6,26},{7,27},{8,28},{9,... | collective-permute-start | bytes 688136 | tf_op jit(solution)/shard_map/ppermute | solution.py:20
  243.0 32.2 %collective-permute-start.17 = (bf16[128,896]{1,0:T(8,128)(2,1)S(1)}, bf16[128,896]{1,0:T(8,128)(2,1)S(1)}, u32[]{:S(2)}, u32[]{:S(2)}) collective-permute-start(bf16[128,896]{1,0:T(8,128)(2,1)S(1)} %get-tuple-element.53), channel_id=1, source_target_pairs={{0,12},{1,13},{2,14},{3,15},{4,16},{5,17},{6,18},{7,19},{8,20},{9,... | collective-permute-start | bytes 688136 | tf_op jit(solution)/shard_map/ppermute | solution.py:20
  246.9 28.3 %collective-permute-start.21 = (bf16[128,896]{1,0:T(8,128)(2,1)S(1)}, bf16[128,896]{1,0:T(8,128)(2,1)S(1)}, u32[]{:S(2)}, u32[]{:S(2)}) collective-permute-start(bf16[128,896]{1,0:T(8,128)(2,1)S(1)} %get-tuple-element.60), channel_id=1, source_target_pairs={{0,16},{1,17},{2,18},{3,19},{4,20},{5,21},{6,22},{7,23},{8,24},{9,... | collective-permute-start | bytes 688136 | tf_op jit(solution)/shard_map/ppermute | solution.py:20
  (32 other events, 129.3 us)

commit v2 on v1

--- a/solution.py
+++ b/solution.py
@@ -9,7 +9,7 @@
 
 BF16, F32 = jnp.bfloat16, jnp.float32
 NX, CORES = 4, 2
-CHUNKS = ((1, -1), (2, -2), (3, -3), (0, 4))
+CHUNKS = ((1, -1, 2, -2), (0, 4, 3, -3))
 VMEM = pl.BlockSpec(memory_space=pltpu.VMEM)
 SMEM = pl.BlockSpec(memory_space=pltpu.SMEM)
 
@@ -31,7 +31,7 @@
     )
 
 
-def call(kernel, outs, specs=None, grid=(), out_specs=None, scratch=(), limit=16, flops=0, moved=0):
+def call(kernel, outs, specs=None, grid=(), out_specs=None, scratch=(), limit=20, flops=0, moved=0):
     return pl.pallas_call(
         kernel,
         grid=grid,
@@ -110,13 +110,18 @@
         out_ref[q] = hidden
 
 
-def down_kernel(held, at_ref, own_ref, other_ref, down_ref, out_ref):
+def down_kernel(held, at_ref, own_ref, other_ref, down_ref, out_ref, h_ref):
     core = at_ref[1]
-    for parts_ref, e in ((own_ref, core), (other_ref, 1 - core)):
-        hidden = parts_ref[...].reshape(4 * held, parts_ref.shape[2])
-        got = jnp.dot(hidden, down_ref[e], preferred_element_type=F32).astype(BF16)
-        for r in range(4):
-            out_ref[r, e] = got[r * held : (r + 1) * held]
+
+    @pl.when(pl.program_id(0) == 0)
+    def _():
+        h_ref[core] = own_ref[...].reshape(4 * held, own_ref.shape[2])
+        h_ref[1 - core] = other_ref[...].reshape(4 * held, own_ref.shape[2])
+
+    hidden = h_ref[pl.program_id(0)]
+    got = jnp.dot(hidden, down_ref[0], preferred_element_type=F32).astype(BF16)
+    for r in range(4):
+        out_ref[r, 0] = got[r * held : (r + 1) * held]
 
 
 def mix_kernel(held, rows, back_ref, code_ref, weight_ref, *outs):
@@ -161,6 +166,10 @@
     def swap_y(value):
         return lax.all_to_all(value, "section", 0, 0, axis_index_groups=y_groups, tiled=True)
 
+    gate_weight, up_weight, down_weight = (
+        pltpu.with_memory_space_constraint(w, pltpu.HBM)
+        for w in (gate_weight, up_weight, down_weight)
+    )
     info = jnp.concatenate([routes.T.astype(BF16), combine.T.astype(BF16)], axis=0)
     block = {0: jnp.concatenate([tokens, jnp.pad(info, ((0, 0), (0, width - rows)))], axis=0)}
     for d in (1, -1, 2, -2, 3, -3, 4):
@@ -200,7 +209,12 @@
         out = call(
             functools.partial(down_kernel, held),
             shape(4, 2, held, width),
-            [SMEM, VMEM, VMEM, VMEM],
+            [SMEM]
+            + [pl.BlockSpec((4, held, units), lambda i: (0, 0, 0))] * 2
+            + [pl.BlockSpec((1, units, width), lambda i: (i, 0, 0))],
+            grid=(2,),
+            out_specs=pl.BlockSpec((4, 1, held, width), lambda i: (0, i, 0, 0)),
+            scratch=[pltpu.VMEM((2, 4 * held, units), BF16)],
             flops=16 * held * width * units,
             moved=6 << 20,
         )(at, parts, others, down_weight)

time: 279 us -> 231 us (0.83)
  the two profiles are of different devices: /device:TPU:66 before, /device:TPU:1 now
where the time goes in v2:
time: 231 us; the launch traced here: 229 us
  waiting for transfers between devices  113 us (49%)
  starting transfers between devices  71 us (31%)
  Pallas kernels  38.8 us (17%)
  local copies, waits for them, and re-layouts  3.48 us (2%)
  other arithmetic  3.35 us (1%)
    ppermute x14, waiting for transfers between devices, along_expert(): lax.ppermute(value, 'expert', [(i, (i // NX + dz) % planes * NX + (i % NX...  43.2 us
    all_to_all x4, waiting for transfers between devices, swap_x(): lax.all_to_all(value, 'expert', 0, 0, axis_index_groups=x_groups, tiled=T...  39.9 us
    all_to_all x4, waiting for transfers between devices, swap_y(): lax.all_to_all(value, 'section', 0, 0, axis_index_groups=y_groups, tiled=...  27.4 us
    ppermute x14, starting transfers between devices, along_expert(): lax.ppermute(value, 'expert', [(i, (i // NX + dz) % planes * NX + (i % NX...  22.1 us
    ppermute x4, starting transfers between devices, along_section(): lax.ppermute(value, 'section', [(i, (i + CORES * dy) % count ^ flip) for...  17.6 us
    all_to_all x4, starting transfers between devices, swap_x(): lax.all_to_all(value, 'expert', 0, 0, axis_index_groups=x_groups, tiled=T...  16.4 us
    pallas_call x2, Pallas kernels, body(): call(functools.partial(up_kernel, held), [shape(4, 2, held, units)] * 2,...  15 us
    all_to_all x4, starting transfers between devices, swap_y(): lax.all_to_all(value, 'section', 0, 0, axis_index_groups=y_groups, tiled=...  14.9 us
  transfers between devices with their start and end apart: 26, of which 15 were waited for; matrix products, arithmetic and copies ran while one was open for 0% of the time, Pallas kernels for 15%

profile of v2, /device:TPU:1, one launch (start us, length us, event | category | flops | bytes accessed | tf_op | source)
XLA Modules:
  0.0 229.3 jit_solution(4437590022504001681)
XLA Ops:
  4.9 4.0 %collective-permute-start.1 = (bf16[144,896]{1,0:T(8,128)(2,1)S(1)}, bf16[144,896]{1,0:T(8,128)(2,1)S(1)}, u32[]{:S(2)}, u32[]{:S(2)}) collective-permute-start(bf16[144,896]{1,0:T(8,128)(2,1)S(1)} %pad_maximum_fusion.refs_0_), channel_id=1, source_target_pairs={{0,28},{1,29},{2,30},{3,31},{4,0},{5,1},{6,2},{7,3},{8,4},{9,5},{1... | collective-permute-start | bytes 774152 | tf_op jit(solution)/shard_map/ppermute | solution.py:20
  8.9 5.9 %collective-permute-done.refs_0_ = bf16[144,896]{1,0:T(8,128)(2,1)S(1)} collective-permute-done((bf16[144,896]{1,0:T(8,128)(2,1)S(1)}, bf16[144,896]{1,0:T(8,128)(2,1)S(1)}, u32[]{:S(2)}, u32[]{:S(2)}) %collective-permute-start) | collective-permute-done | bytes 258080 | tf_op jit(solution)/shard_map/ppermute | solution.py:20
  17.5 5.0 %collective-permute-done.2.refs_2_ = bf16[144,896]{1,0:T(8,128)(2,1)} collective-permute-done((bf16[144,896]{1,0:T(8,128)(2,1)S(1)}, bf16[144,896]{1,0:T(8,128)(2,1)}, u32[]{:S(2)}, u32[]{:S(2)}) %collective-permute-start.2) | collective-permute-done | bytes 258080 | tf_op jit(solution)/shard_map/ppermute | solution.py:20
  25.9 4.0 %all-to-all-start = ((bf16[4,192,896]{2,1,0:T(8,128)(2,1)}), bf16[4,192,896]{2,1,0:T(8,128)(2,1)S(1)}, u32[]{:S(2)}, u32[]{:S(2)}) async-start(bf16[4,192,896]{2,1,0:T(8,128)(2,1)} %get-tuple-element.23), calls=%async_computation | async-start | bytes 2752512 | tf_op jit(solution)/shard_map/all_to_all | solution.py:164
  29.9 16.2 %all-to-all-done.rows_ref = bf16[4,192,896]{2,1,0:T(8,128)(2,1)S(1)} async-done(((bf16[4,192,896]{2,1,0:T(8,128)(2,1)}), bf16[4,192,896]{2,1,0:T(8,128)(2,1)S(1)}, u32[]{:S(2)}, u32[]{:S(2)}) %all-to-all-start) | async-done | bytes 1376288 | tf_op jit(solution)/shard_map/all_to_all | solution.py:164
  46.1 7.3 %shard_map.65 = (bf16[4,2,96,1024]{3,2,1,0:T(8,128)(2,1)S(1)}, bf16[4,2,96,1024]{3,2,1,0:T(8,128)(2,1)}) custom-call(s32[2]{0:T(128)S(1)} %pad_add_fusion.at_ref, bf16[4,192,896]{2,1,0:T(8,128)(2,1)S(1)} %all-to-all-done.rows_ref, bf16[2,896,1024]{2,1,0:T(8,128)(2,1)} %gate_ref.3, bf16[2,896,1024]{2,1,0:T(8,128)(2,1)} %up_ref.3), custom_call_target="tpu_custom_call" | custom-call | flops 2818572288 | bytes 10485760 | tf_op jit(solution)/shard_map/pallas_call | solution.py:192
  59.2 5.6 %collective-permute-done.12.refs_3_ = bf16[144,896]{1,0:T(8,128)(2,1)S(1)} collective-permute-done((bf16[144,896]{1,0:T(8,128)(2,1)S(1)}, bf16[144,896]{1,0:T(8,128)(2,1)S(1)}, u32[]{:S(2)}, u32[]{:S(2)}) %collective-permute-start.12) | collective-permute-done | bytes 258080 | tf_op jit(solution)/shard_map/ppermute | solution.py:20
  72.4 4.3 %all-to-all-start.4 = ((bf16[4,192,896]{2,1,0:T(8,128)(2,1)}), bf16[4,192,896]{2,1,0:T(8,128)(2,1)}, u32[]{:S(2)}, u32[]{:S(2)}) async-start(bf16[4,192,896]{2,1,0:T(8,128)(2,1)} %copy-done.2), calls=%async_computation.4 | async-start | bytes 2752512 | tf_op jit(solution)/shard_map/all_to_all | solution.py:164
  78.2 16.0 %all-to-all-done.4.rows_ref = bf16[4,192,896]{2,1,0:T(8,128)(2,1)} async-done(((bf16[4,192,896]{2,1,0:T(8,128)(2,1)}), bf16[4,192,896]{2,1,0:T(8,128)(2,1)}, u32[]{:S(2)}, u32[]{:S(2)}) %all-to-all-start.4) | async-done | bytes 1376288 | tf_op jit(solution)/shard_map/all_to_all | solution.py:164
  94.2 4.2 %all-to-all-start.1 = ((bf16[4,2,96,1024]{3,2,1,0:T(8,128)(2,1)}), bf16[4,2,96,1024]{3,2,1,0:T(8,128)(2,1)S(1)}, u32[]{:S(2)}, u32[]{:S(2)}) async-start(bf16[4,2,96,1024]{3,2,1,0:T(8,128)(2,1)} %shard_map.66), calls=%async_computation.1 | async-start | bytes 3145728 | tf_op jit(solution)/shard_map/all_to_all | solution.py:167
  98.4 7.7 %shard_map.71 = (bf16[4,2,96,1024]{3,2,1,0:T(8,128)(2,1)S(1)}, bf16[4,2,96,1024]{3,2,1,0:T(8,128)(2,1)}) custom-call(s32[2]{0:T(128)S(1)} %pad_add_fusion.at_ref, bf16[4,192,896]{2,1,0:T(8,128)(2,1)} %all-to-all-done.4.rows_ref, bf16[2,896,1024]{2,1,0:T(8,128)(2,1)} %gate_ref.3, bf16[2,896,1024]{2,1,0:T(8,128)(2,1)} %up_ref.3), custom_call_target="tpu_custom_call" | custom-call | flops 2818572288 | bytes 10485760 | tf_op jit(solution)/shard_map/pallas_call | solution.py:192
  109.7 7.1 %all-to-all-done.1.terms_ref = bf16[4,2,96,1024]{3,2,1,0:T(8,128)(2,1)S(1)} async-done(((bf16[4,2,96,1024]{3,2,1,0:T(8,128)(2,1)}), bf16[4,2,96,1024]{3,2,1,0:T(8,128)(2,1)S(1)}, u32[]{:S(2)}, u32[]{:S(2)}) %all-to-all-start.1) | async-done | bytes 1572896 | tf_op jit(solution)/shard_map/all_to_all | solution.py:167
  117.9 3.6 %all-to-all-start.2 = ((bf16[4,96,1024]{2,1,0:T(8,128)(2,1)}), bf16[4,96,1024]{2,1,0:T(8,128)(2,1)S(1)}, u32[]{:S(2)}, u32[]{:S(2)}) async-start(bf16[4,96,1024]{2,1,0:T(8,128)(2,1)} %shard_map.67), calls=%async_computation.2 | async-start | bytes 1572864 | tf_op jit(solution)/shard_map/all_to_all | solution.py:167
  124.5 5.7 %all-to-all-done.2.own_ref = bf16[4,96,1024]{2,1,0:T(8,128)(2,1)S(1)} async-done(((bf16[4,96,1024]{2,1,0:T(8,128)(2,1)}), bf16[4,96,1024]{2,1,0:T(8,128)(2,1)S(1)}, u32[]{:S(2)}, u32[]{:S(2)}) %all-to-all-start.2) | async-done | bytes 786464 | tf_op jit(solution)/shard_map/all_to_all | solution.py:167
  133.7 4.8 %collective-permute-start.5 = (bf16[4,96,1024]{2,1,0:T(8,128)(2,1)S(1)}, bf16[4,96,1024]{2,1,0:T(8,128)(2,1)}, u32[]{:S(2)}, u32[]{:S(2)}) collective-permute-start(bf16[4,96,1024]{2,1,0:T(8,128)(2,1)S(1)} %all-to-all-done.2.own_ref), channel_id=1, source_target_pairs={{0,32},{32,0},{64,96},{96,64},{128,160},{160,128},{192,224},{224,1... | collective-permute-start | bytes 2359304 | tf_op jit(solution)/shard_map/ppermute | solution.py:29
  138.6 11.1 %all-to-all-done.5.terms_ref = bf16[4,2,96,1024]{3,2,1,0:T(8,128)(2,1)S(1)} async-done(((bf16[4,2,96,1024]{3,2,1,0:T(8,128)(2,1)}), bf16[4,2,96,1024]{3,2,1,0:T(8,128)(2,1)S(1)}, u32[]{:S(2)}, u32[]{:S(2)}) %all-to-all-start.5) | async-done | bytes 1572896 | tf_op jit(solution)/shard_map/all_to_all | solution.py:167
  154.3 4.7 %shard_map.68 = bf16[4,2,96,896]{3,2,1,0:T(8,128)(2,1)} custom-call(s32[2]{0:T(128)S(1)} %pad_add_fusion.at_ref, bf16[4,96,1024]{2,1,0:T(8,128)(2,1)S(1)} %all-to-all-done.2.own_ref, bf16[4,96,1024]{2,1,0:T(8,128)(2,1)} %collective-permute-done.5.other_ref, bf16[2,1024,896]{2,1,0:T(8,128)(2,1)} %down_ref.3), custom_call_target="tpu_custom_call" | custom-call | flops 1409286144 | bytes 6291456 | tf_op jit(solution)/shard_map/pallas_call | solution.py:209
  166.1 7.0 %collective-permute-start.14 = (bf16[4,96,1024]{2,1,0:T(8,128)(2,1)S(1)}, bf16[4,96,1024]{2,1,0:T(8,128)(2,1)S(1)}, u32[]{:S(2)}, u32[]{:S(2)}) collective-permute-start(bf16[4,96,1024]{2,1,0:T(8,128)(2,1)S(1)} %all-to-all-done.6.own_ref), channel_id=1, source_target_pairs={{0,32},{32,0},{64,96},{96,64},{128,160},{160,128},{192,224},{224,1... | collective-permute-start | bytes 2359304 | tf_op jit(solution)/shard_map/ppermute | solution.py:29
  175.0 4.5 %shard_map.74 = bf16[4,2,96,896]{3,2,1,0:T(8,128)(2,1)} custom-call(s32[2]{0:T(128)S(1)} %pad_add_fusion.at_ref, bf16[4,96,1024]{2,1,0:T(8,128)(2,1)S(1)} %all-to-all-done.6.own_ref, bf16[4,96,1024]{2,1,0:T(8,128)(2,1)S(1)} %collective-permute-done.14.other_ref, bf16[2,1024,896]{2,1,0:T(8,128)(2,1)} %down_ref.3), custom_call_target="tpu_custom_call" | custom-call | flops 1409286144 | bytes 6291456 | tf_op jit(solution)/shard_map/pallas_call | solution.py:209
  179.5 4.5 %all-to-all-start.7 = ((bf16[4,2,96,896]{3,2,1,0:T(8,128)(2,1)}), bf16[4,2,96,896]{3,2,1,0:T(8,128)(2,1)S(1)}, u32[]{:S(2)}, u32[]{:S(2)}) async-start(bf16[4,2,96,896]{3,2,1,0:T(8,128)(2,1)} %shard_map.74), calls=%async_computation.7 | async-start | bytes 2752512 | tf_op jit(solution)/shard_map/all_to_all | solution.py:164
  189.5 7.8 %all-to-all-done.7.back_ref = bf16[4,2,96,896]{3,2,1,0:T(8,128)(2,1)S(1)} async-done(((bf16[4,2,96,896]{3,2,1,0:T(8,128)(2,1)}), bf16[4,2,96,896]{3,2,1,0:T(8,128)(2,1)S(1)}, u32[]{:S(2)}, u32[]{:S(2)}) %all-to-all-start.7) | async-done | bytes 1376288 | tf_op jit(solution)/shard_map/all_to_all | solution.py:164
  205.0 5.4 %collective-permute-done.15 = bf16[128,896]{1,0:T(8,128)(2,1)S(1)} collective-permute-done((bf16[128,896]{1,0:T(8,128)(2,1)S(1)}, bf16[128,896]{1,0:T(8,128)(2,1)S(1)}, u32[]{:S(2)}, u32[]{:S(2)}) %collective-permute-start.15) | collective-permute-done | bytes 229408 | tf_op jit(solution)/shard_map/ppermute | solution.py:20
  210.4 8.1 %collective-permute-done.16 = bf16[128,896]{1,0:T(8,128)(2,1)S(1)} collective-permute-done((bf16[128,896]{1,0:T(8,128)(2,1)S(1)}, bf16[128,896]{1,0:T(8,128)(2,1)S(1)}, u32[]{:S(2)}, u32[]{:S(2)}) %collective-permute-start.16) | collective-permute-done | bytes 229408 | tf_op jit(solution)/shard_map/ppermute | solution.py:20
  218.5 9.9 %collective-permute-done.17 = bf16[128,896]{1,0:T(8,128)(2,1)S(1)} collective-permute-done((bf16[128,896]{1,0:T(8,128)(2,1)S(1)}, bf16[128,896]{1,0:T(8,128)(2,1)S(1)}, u32[]{:S(2)}, u32[]{:S(2)}) %collective-permute-start.17) | collective-permute-done | bytes 229408 | tf_op jit(solution)/shard_map/ppermute | solution.py:20
  (72 shorter events, 64.9 us)
Async XLA Ops:
  2.4 12.4 %collective-permute-start = (bf16[144,896]{1,0:T(8,128)(2,1)S(1)}, bf16[144,896]{1,0:T(8,128)(2,1)S(1)}, u32[]{:S(2)}, u32[]{:S(2)}) collective-permute-start(bf16[144,896]{1,0:T(8,128)(2,1)S(1)} %pad_maximum_fusion.refs_0_), channel_id=1, source_target_pairs={{0,4},{1,5},{2,6},{3,7},{4,8},{5,9},{6,10},{7,11},{8,12},{9,13},{1... | collective-permute-start | bytes 774152 | tf_op jit(solution)/shard_map/ppermute | solution.py:20
  4.9 9.9 %collective-permute-start.1 = (bf16[144,896]{1,0:T(8,128)(2,1)S(1)}, bf16[144,896]{1,0:T(8,128)(2,1)S(1)}, u32[]{:S(2)}, u32[]{:S(2)}) collective-permute-start(bf16[144,896]{1,0:T(8,128)(2,1)S(1)} %pad_maximum_fusion.refs_0_), channel_id=1, source_target_pairs={{0,28},{1,29},{2,30},{3,31},{4,0},{5,1},{6,2},{7,3},{8,4},{9,5},{1... | collective-permute-start | bytes 774152 | tf_op jit(solution)/shard_map/ppermute | solution.py:20
  25.9 20.2 %all-to-all-start = ((bf16[4,192,896]{2,1,0:T(8,128)(2,1)}), bf16[4,192,896]{2,1,0:T(8,128)(2,1)S(1)}, u32[]{:S(2)}, u32[]{:S(2)}) async-start(bf16[4,192,896]{2,1,0:T(8,128)(2,1)} %get-tuple-element.23), calls=%async_computation | async-start | bytes 2752512 | tf_op jit(solution)/shard_map/all_to_all | solution.py:164
  29.9 29.2 %collective-permute-start.10 = (bf16[144,896]{1,0:T(8,128)(2,1)}, bf16[144,896]{1,0:T(8,128)(2,1)}, u32[]{:S(2)}, u32[]{:S(2)}) collective-permute-start(bf16[144,896]{1,0:T(8,128)(2,1)} %collective-permute-done.2.refs_2_), channel_id=1, source_target_pairs={{0,4},{1,5},{2,6},{3,7},{4,8},{5,9},{6,10},{7,11},{8,12},{9,13},{1... | collective-permute-start | bytes 774152 | tf_op jit(solution)/shard_map/ppermute | solution.py:20
  53.4 23.3 %collective-permute-start.4 = (bf16[4,2,96,1024]{3,2,1,0:T(8,128)(2,1)}, bf16[4,2,96,1024]{3,2,1,0:T(8,128)(2,1)S(1)}, u32[]{:S(2)}, u32[]{:S(2)}) collective-permute-start(bf16[4,2,96,1024]{3,2,1,0:T(8,128)(2,1)} %get-tuple-element.25), channel_id=1, source_target_pairs={{0,32},{32,0},{64,96},{96,64},{128,160},{160,128},{192,224},{224,1... | collective-permute-start | bytes 4718600 | tf_op jit(solution)/shard_map/ppermute | solution.py:29
  56.8 7.9 %collective-permute-start.12 = (bf16[144,896]{1,0:T(8,128)(2,1)S(1)}, bf16[144,896]{1,0:T(8,128)(2,1)S(1)}, u32[]{:S(2)}, u32[]{:S(2)}) collective-permute-start(bf16[144,896]{1,0:T(8,128)(2,1)S(1)} %copy-done.4), channel_id=1, source_target_pairs={{0,28},{1,29},{2,30},{3,31},{4,0},{5,1},{6,2},{7,3},{8,4},{9,5},{1... | collective-permute-start | bytes 774152 | tf_op jit(solution)/shard_map/ppermute | solution.py:20
  59.2 8.9 %collective-permute-start.11 = (bf16[144,896]{1,0:T(8,128)(2,1)}, bf16[144,896]{1,0:T(8,128)(2,1)S(1)}, u32[]{:S(2)}, u32[]{:S(2)}) collective-permute-start(bf16[144,896]{1,0:T(8,128)(2,1)} %collective-permute-done.10.refs_2_), channel_id=1, source_target_pairs={{0,4},{1,5},{2,6},{3,7},{4,8},{5,9},{6,10},{7,11},{8,12},{9,13},{1... | collective-permute-start | bytes 774152 | tf_op jit(solution)/shard_map/ppermute | solution.py:20
  72.4 21.8 %all-to-all-start.4 = ((bf16[4,192,896]{2,1,0:T(8,128)(2,1)}), bf16[4,192,896]{2,1,0:T(8,128)(2,1)}, u32[]{:S(2)}, u32[]{:S(2)}) async-start(bf16[4,192,896]{2,1,0:T(8,128)(2,1)} %copy-done.2), calls=%async_computation.4 | async-start | bytes 2752512 | tf_op jit(solution)/shard_map/all_to_all | solution.py:164
  94.2 22.5 %all-to-all-start.1 = ((bf16[4,2,96,1024]{3,2,1,0:T(8,128)(2,1)}), bf16[4,2,96,1024]{3,2,1,0:T(8,128)(2,1)S(1)}, u32[]{:S(2)}, u32[]{:S(2)}) async-start(bf16[4,2,96,1024]{3,2,1,0:T(8,128)(2,1)} %shard_map.66), calls=%async_computation.1 | async-start | bytes 3145728 | tf_op jit(solution)/shard_map/all_to_all | solution.py:167
  107.3 14.2 %collective-permute-start.13 = (bf16[4,2,96,1024]{3,2,1,0:T(8,128)(2,1)}, bf16[4,2,96,1024]{3,2,1,0:T(8,128)(2,1)}, u32[]{:S(2)}, u32[]{:S(2)}) collective-permute-start(bf16[4,2,96,1024]{3,2,1,0:T(8,128)(2,1)} %get-tuple-element.34), channel_id=1, source_target_pairs={{0,32},{32,0},{64,96},{96,64},{128,160},{160,128},{192,224},{224,1... | collective-permute-start | bytes 4718600 | tf_op jit(solution)/shard_map/ppermute | solution.py:29
  117.9 12.3 %all-to-all-start.2 = ((bf16[4,96,1024]{2,1,0:T(8,128)(2,1)}), bf16[4,96,1024]{2,1,0:T(8,128)(2,1)S(1)}, u32[]{:S(2)}, u32[]{:S(2)}) async-start(bf16[4,96,1024]{2,1,0:T(8,128)(2,1)} %shard_map.67), calls=%async_computation.2 | async-start | bytes 1572864 | tf_op jit(solution)/shard_map/all_to_all | solution.py:167
  130.2 19.4 %all-to-all-start.5 = ((bf16[4,2,96,1024]{3,2,1,0:T(8,128)(2,1)}), bf16[4,2,96,1024]{3,2,1,0:T(8,128)(2,1)S(1)}, u32[]{:S(2)}, u32[]{:S(2)}) async-start(bf16[4,2,96,1024]{3,2,1,0:T(8,128)(2,1)} %shard_map.72), calls=%async_computation.5 | async-start | bytes 3145728 | tf_op jit(solution)/shard_map/all_to_all | solution.py:167
  133.7 20.5 %collective-permute-start.5 = (bf16[4,96,1024]{2,1,0:T(8,128)(2,1)S(1)}, bf16[4,96,1024]{2,1,0:T(8,128)(2,1)}, u32[]{:S(2)}, u32[]{:S(2)}) collective-permute-start(bf16[4,96,1024]{2,1,0:T(8,128)(2,1)S(1)} %all-to-all-done.2.own_ref), channel_id=1, source_target_pairs={{0,32},{32,0},{64,96},{96,64},{128,160},{160,128},{192,224},{224,1... | collective-permute-start | bytes 2359304 | tf_op jit(solution)/shard_map/ppermute | solution.py:29
  150.7 11.8 %all-to-all-start.6 = ((bf16[4,96,1024]{2,1,0:T(8,128)(2,1)}), bf16[4,96,1024]{2,1,0:T(8,128)(2,1)S(1)}, u32[]{:S(2)}, u32[]{:S(2)}) async-start(bf16[4,96,1024]{2,1,0:T(8,128)(2,1)} %shard_map.73), calls=%async_computation.6 | async-start | bytes 1572864 | tf_op jit(solution)/shard_map/all_to_all | solution.py:167
  162.5 16.9 %all-to-all-start.3 = ((bf16[4,2,96,896]{3,2,1,0:T(8,128)(2,1)}), bf16[4,2,96,896]{3,2,1,0:T(8,128)(2,1)S(1)}, u32[]{:S(2)}, u32[]{:S(2)}) async-start(bf16[4,2,96,896]{3,2,1,0:T(8,128)(2,1)} %shard_map.68), calls=%async_computation.3 | async-start | bytes 2752512 | tf_op jit(solution)/shard_map/all_to_all | solution.py:164
  166.1 8.9 %collective-permute-start.14 = (bf16[4,96,1024]{2,1,0:T(8,128)(2,1)S(1)}, bf16[4,96,1024]{2,1,0:T(8,128)(2,1)S(1)}, u32[]{:S(2)}, u32[]{:S(2)}) collective-permute-start(bf16[4,96,1024]{2,1,0:T(8,128)(2,1)S(1)} %all-to-all-done.6.own_ref), channel_id=1, source_target_pairs={{0,32},{32,0},{64,96},{96,64},{128,160},{160,128},{192,224},{224,1... | collective-permute-start | bytes 2359304 | tf_op jit(solution)/shard_map/ppermute | solution.py:29
  179.5 17.7 %all-to-all-start.7 = ((bf16[4,2,96,896]{3,2,1,0:T(8,128)(2,1)}), bf16[4,2,96,896]{3,2,1,0:T(8,128)(2,1)S(1)}, u32[]{:S(2)}, u32[]{:S(2)}) async-start(bf16[4,2,96,896]{3,2,1,0:T(8,128)(2,1)} %shard_map.74), calls=%async_computation.7 | async-start | bytes 2752512 | tf_op jit(solution)/shard_map/all_to_all | solution.py:164
  185.6 16.1 %collective-permute-start.6 = (bf16[128,896]{1,0:T(8,128)(2,1)}, bf16[128,896]{1,0:T(8,128)(2,1)S(1)}, u32[]{:S(2)}, u32[]{:S(2)}) collective-permute-start(bf16[128,896]{1,0:T(8,128)(2,1)} %get-tuple-element.28), channel_id=1, source_target_pairs={{0,28},{1,29},{2,30},{3,31},{4,0},{5,1},{6,2},{7,3},{8,4},{9,5},{1... | collective-permute-start | bytes 688136 | tf_op jit(solution)/shard_map/ppermute | solution.py:20
  186.8 15.6 %collective-permute-start.7 = (bf16[128,896]{1,0:T(8,128)(2,1)S(1)}, bf16[128,896]{1,0:T(8,128)(2,1)S(1)}, u32[]{:S(2)}, u32[]{:S(2)}) collective-permute-start(bf16[128,896]{1,0:T(8,128)(2,1)S(1)} %get-tuple-element.29), channel_id=1, source_target_pairs={{0,4},{1,5},{2,6},{3,7},{4,8},{5,9},{6,10},{7,11},{8,12},{9,13},{1... | collective-permute-start | bytes 688136 | tf_op jit(solution)/shard_map/ppermute | solution.py:20
  187.1 17.9 %collective-permute-start.8 = (bf16[128,896]{1,0:T(8,128)(2,1)S(1)}, bf16[128,896]{1,0:T(8,128)(2,1)S(1)}, u32[]{:S(2)}, u32[]{:S(2)}) collective-permute-start(bf16[128,896]{1,0:T(8,128)(2,1)S(1)} %get-tuple-element.30), channel_id=1, source_target_pairs={{0,24},{1,25},{2,26},{3,27},{4,28},{5,29},{6,30},{7,31},{8,0},{9,1... | collective-permute-start | bytes 688136 | tf_op jit(solution)/shard_map/ppermute | solution.py:20
  188.3 16.7 %collective-permute-start.9 = (bf16[128,896]{1,0:T(8,128)(2,1)S(1)}, bf16[128,896]{1,0:T(8,128)(2,1)S(1)}, u32[]{:S(2)}, u32[]{:S(2)}) collective-permute-start(bf16[128,896]{1,0:T(8,128)(2,1)S(1)} %get-tuple-element.31), channel_id=1, source_target_pairs={{0,8},{1,9},{2,10},{3,11},{4,12},{5,13},{6,14},{7,15},{8,16},{9,17... | collective-permute-start | bytes 688136 | tf_op jit(solution)/shard_map/ppermute | solution.py:20
  198.2 12.2 %collective-permute-start.15 = (bf16[128,896]{1,0:T(8,128)(2,1)S(1)}, bf16[128,896]{1,0:T(8,128)(2,1)S(1)}, u32[]{:S(2)}, u32[]{:S(2)}) collective-permute-start(bf16[128,896]{1,0:T(8,128)(2,1)S(1)} %get-tuple-element.38), channel_id=1, source_target_pairs={{0,16},{1,17},{2,18},{3,19},{4,20},{5,21},{6,22},{7,23},{8,24},{9,... | collective-permute-start | bytes 688136 | tf_op jit(solution)/shard_map/ppermute | solution.py:20
  201.7 16.8 %collective-permute-start.16 = (bf16[128,896]{1,0:T(8,128)(2,1)S(1)}, bf16[128,896]{1,0:T(8,128)(2,1)S(1)}, u32[]{:S(2)}, u32[]{:S(2)}) collective-permute-start(bf16[128,896]{1,0:T(8,128)(2,1)S(1)} %get-tuple-element.39), channel_id=1, source_target_pairs={{0,20},{1,21},{2,22},{3,23},{4,24},{5,25},{6,26},{7,27},{8,28},{9,... | collective-permute-start | bytes 688136 | tf_op jit(solution)/shard_map/ppermute | solution.py:20
  202.3 26.1 %collective-permute-start.17 = (bf16[128,896]{1,0:T(8,128)(2,1)S(1)}, bf16[128,896]{1,0:T(8,128)(2,1)S(1)}, u32[]{:S(2)}, u32[]{:S(2)}) collective-permute-start(bf16[128,896]{1,0:T(8,128)(2,1)S(1)} %get-tuple-element.40), channel_id=1, source_target_pairs={{0,12},{1,13},{2,14},{3,15},{4,16},{5,17},{6,18},{7,19},{8,20},{9,... | collective-permute-start | bytes 688136 | tf_op jit(solution)/shard_map/ppermute | solution.py:20
  (15 other events, 127.3 us)

commit v3 on v1

v3 whole, which is shorter than its diff:
```python
import functools

import jax
import jax.numpy as jnp
from jax import lax
from jax.experimental import pallas as pl
from jax.experimental.pallas import tpu as pltpu
from jax.sharding import PartitionSpec as P

BF16, F32 = jnp.bfloat16, jnp.float32
NX, CORES = 4, 2
CHUNKS = ((1, -1, 2, -2), (0, 4, 3, -3))
VMEM = pl.BlockSpec(memory_space=pltpu.VMEM)
SMEM = pl.BlockSpec(memory_space=pltpu.SMEM)
HBM = pl.BlockSpec(memory_space=pltpu.HBM)


def along_expert(value, dz, dx):
    count = lax.axis_size("expert")
    planes = count // NX
    return lax.ppermute(
        value,
        "expert",
        [(i, (i // NX + dz) % planes * NX + (i % NX + dx) % NX) for i in range(count)],
    )


def along_section(value, dy, flip):
    count = lax.axis_size("section")
    return lax.ppermute(
        value, "section", [(i, (i + CORES * dy) % count ^ flip) for i in range(count)]
    )


def call(kernel, outs, specs=None, grid=(), out_specs=None, scratch=(), limit=20, flops=0, moved=0):
    return pl.pallas_call(
        kernel,
        grid=grid,
        out_shape=outs,
        in_specs=specs,
        out_specs=out_specs or jax.tree.map(lambda _: VMEM, outs),
        scratch_shapes=scratch,
        compiler_params=pltpu.CompilerParams(vmem_limit_bytes=limit << 20),
        cost_estimate=pl.CostEstimate(flops=16 * flops, bytes_accessed=16 * moved, transcendentals=0),
    )


def select_kernel(capacity, rows, at_ref, *refs):
    nz = len(refs) - 3
    blocks, (out_ref, code_ref, weight_ref) = refs[:nz], refs[nz:]
    per_plane = 2 * NX
    row = lax.broadcasted_iota(jnp.int32, (per_plane, rows), 0)
    expert = (at_ref[0] * per_plane + row).astype(F32)
    earlier = (
        lax.broadcasted_iota(jnp.int32, (rows, rows), 0)
        < lax.broadcasted_iota(jnp.int32, (rows, rows), 1)
    ).astype(F32).astype(BF16)
    codes = []
    for n, block in enumerate(blocks):
        info = block[pl.ds(rows, 16), pl.ds(0, rows)].astype(F32)
        named = jnp.zeros((per_plane, rows), F32)
        weight = jnp.zeros((per_plane, rows), F32)
        for k in range(8):
            hit = info[k : k + 1] == expert
            named = named + jnp.where(hit, 1.0, 0.0)
            weight = weight + jnp.where(hit, info[8 + k : 9 + k], 0.0)
        slot = jnp.dot(named.astype(BF16), earlier, preferred_element_type=F32)
        codes.append(jnp.where(named > 0.5, slot + float(n * capacity), -1.0))
        weight_ref[:, pl.ds(n * rows, rows)] = weight
    code = jnp.concatenate(codes, axis=1)
    code_ref[...] = code
    held = nz * capacity
    at = lax.broadcasted_iota(jnp.int32, (held, nz * rows), 0).astype(F32)
    tokens = jnp.concatenate([block[pl.ds(0, rows), :] for block in blocks], axis=0)
    for r in range(NX):
        pick = jnp.concatenate(
            [jnp.where(at == code[2 * r + e : 2 * r + e + 1], 1.0, 0.0) for e in range(2)], axis=0
        ).astype(BF16)
        out_ref[r] = jnp.dot(pick, tokens, preferred_element_type=F32).astype(BF16)


def up_kernel(held, flip, at_ref, rows_ref, gate_ref, up_ref, out_ref, x_ref, w_ref, sems):
    y = at_ref[2]
    expert = (at_ref[1] + flip) % 2
    half = gate_ref.shape[2] // 2
    pieces = [(part, c) for c in range(2) for part in range(2)]

    def fetch(n):
        part, c = pieces[n]
        return pltpu.make_async_copy(
            (gate_ref, up_ref)[part].at[expert, :, pl.ds(c * half, half)], w_ref.at[n], sems.at[n]
        )

    for n in range(4):
        fetch(n).start()
    for r in range(4):
        x_ref[pl.ds(r * held, held), :] = rows_ref[r, pl.ds(pl.multiple_of(expert * held, held), held), :]
    for n, (part, c) in enumerate(pieces):
        fetch(n).wait()
        sums = jnp.dot(x_ref[...], w_ref[n], preferred_element_type=F32).astype(BF16)
        for r in range(4):
            out_ref[(r + 4 - y) % 4, part, :, pl.ds(c * half, half)] = sums[
                r * held : (r + 1) * held
            ]


def join_kernel(keep_ref, got_ref, *outs):
    for q in range(4):
        outs[q][...] = (keep_ref[q].astype(F32) + got_ref[q].astype(F32)).astype(BF16)


def silu_kernel(a_ref, b_ref, c_ref, d_ref, out_ref):
    gate, up = (
        (a_ref[i].astype(F32) + b_ref[i].astype(F32)) + (c_ref[i].astype(F32) + d_ref[i].astype(F32))
        for i in range(2)
    )
    out_ref[...] = (jax.nn.silu(gate) * up).astype(BF16)


def down_kernel(held, at_ref, own_ref, other_ref, down_ref, out_ref, w_ref, sems):
    core, y = at_ref[1], at_ref[2]

    def fetch(n):
        return pltpu.make_async_copy(down_ref.at[(core + n) % 2], w_ref.at[n], sems.at[n])

    for n in range(2):
        fetch(n).start()
    for n, parts_ref in enumerate((own_ref, other_ref)):
        hidden = parts_ref[...].reshape(4 * held, parts_ref.shape[2])
        fetch(n).wait()
        got = jnp.dot(hidden, w_ref[n], preferred_element_type=F32).astype(BF16)
        for q in range(4):
            out_ref[(y + 4 - q) % 4, (core + n) % 2] = got[q * held : (q + 1) * held]


def mix_kernel(held, rows, back_ref, code_ref, weight_ref, *outs):
    width = code_ref.shape[1]
    at = lax.broadcasted_iota(jnp.int32, (held, width), 0).astype(F32)
    share = jnp.concatenate(
        [
            jnp.where(at == code_ref[j : j + 1, :], weight_ref[j : j + 1, :], 0.0)
            for j in range(2 * NX)
        ],
        axis=0,
    ).astype(BF16)
    total = lax.dot_general(
        share,
        back_ref[...].reshape(share.shape[0], back_ref.shape[3]),
        (((0,), (0,)), ((), ())),
        preferred_element_type=F32,
    ).astype(BF16)
    for n, out in enumerate(outs):
        out[...] = total[n * rows : (n + 1) * rows]


def shape(*dims, dtype=BF16):
    return jax.ShapeDtypeStruct(dims, dtype)


def body(tokens, routes, combine, gate_weight, up_weight, down_weight):
    groups = lax.axis_size("expert")
    per_device, width, units = gate_weight.shape
    rows, fanout = routes.shape
    capacity = 3 * rows * fanout // (2 * per_device * groups)
    place, part = lax.axis_index("expert"), lax.axis_index("section")
    at = jnp.stack([place // NX, part % CORES, part // CORES]).astype(jnp.int32)
    planes = groups // NX
    x_groups = [[z * NX + x for x in range(NX)] for z in range(planes)]
    def swap_x(value):
        return lax.all_to_all(value, "expert", 0, 0, axis_index_groups=x_groups, tiled=True)

    gate_weight, up_weight, down_weight = (
        pltpu.with_memory_space_constraint(w, pltpu.HBM)
        for w in (gate_weight, up_weight, down_weight)
    )
    info = jnp.concatenate([routes.T.astype(BF16), combine.T.astype(BF16)], axis=0)
    block = {0: jnp.concatenate([tokens, jnp.pad(info, ((0, 0), (0, width - rows)))], axis=0)}
    for d in (1, -1, 2, -2, 3, -3, 4):
        step = 1 if d > 0 else -1
        block[d] = along_expert(block[d - step], step, 0)

    chosen = []
    for chunk in CHUNKS:
        nz = len(chunk)
        held = nz * capacity
        chosen.append(
            call(
                functools.partial(select_kernel, capacity, rows),
                [shape(4, 2 * held, width)] + [shape(2 * NX, nz * rows, dtype=F32)] * 2,
                [SMEM] + [VMEM] * nz,
                flops=16 * held * nz * rows * width,
                moved=2 << 20,
            )(at, *[block[d] for d in chunk])
        )

    def expand(came, nz):
        held = nz * capacity
        send, keep = (
            call(
                functools.partial(up_kernel, held, flip),
                shape(4, 2, held, units),
                [SMEM, VMEM, HBM, HBM],
                scratch=[
                    pltpu.VMEM((4 * held, width), BF16),
                    pltpu.VMEM((4, width, units // 2), BF16),
                    pltpu.SemaphoreType.DMA((4,)),
                ],
                flops=16 * held * width * units,
                moved=6 << 20,
            )(at, came, gate_weight, up_weight)
            for flip in (1, 0)
        )
        got = along_section(send, 0, 1)
        return call(
            join_kernel, [shape(2, held, units)] * 4, [VMEM] * 2, moved=3 << 20
        )(keep, got)

    def contract(terms, nz):
        held = nz * capacity
        hidden = call(silu_kernel, shape(held, units), [VMEM] * 4, moved=1 << 20)(*terms)
        parts = jnp.stack([along_section(hidden, q, 0) if q else hidden for q in range(4)])
        others = along_section(parts, 0, 1)
        return call(
            functools.partial(down_kernel, held),
            shape(4, 2, held, width),
            [SMEM, VMEM, VMEM, HBM],
            scratch=[pltpu.VMEM((2, units, width), BF16), pltpu.SemaphoreType.DMA((2,))],
            flops=16 * held * width * units,
            moved=6 << 20,
        )(at, parts, others, down_weight)

    def spread(sums):
        return [along_section(sums[q], q, 0) if q else sums[q] for q in range(4)]

    sizes = [len(chunk) for chunk in CHUNKS]
    came = [swap_x(picked) for picked, _, _ in chosen]
    came[0], chosen = lax.optimization_barrier((came[0], chosen))
    terms = []
    for i, nz in enumerate(sizes):
        if i:
            came[i], sums = lax.optimization_barrier((came[i], sums))
        sums = expand(came[i], nz)
        if i:
            terms[i - 1], sums = lax.optimization_barrier((terms[i - 1], sums))
        terms.append(spread(sums))
    partials = []
    for chunk, (_, code, weight), t in zip(CHUNKS, chosen, terms):
        nz = len(chunk)
        back = swap_x(contract(t, nz))
        mixed = call(
            functools.partial(mix_kernel, nz * capacity, rows),
            [shape(rows, width)] * nz,
            [VMEM] * 3,
            flops=16 * nz * capacity * nz * rows * width,
            moved=2 << 20,
        )(back, code, weight)
        partials += [along_expert(m, -d, 0) if d else m for d, m in zip(chunk, mixed)]
    return sum(p.astype(F32) for p in partials).astype(BF16)


def solution(mesh):
    return jax.shard_map(
        body,
        mesh=mesh,
        in_specs=(
            P("expert", "section"),
            P("expert", None),
            P("expert", None),
            P("expert", "section", None),
            P("expert", "section", None),
            P("expert", None, "section"),
        ),
        out_specs=P("expert", "section"),
        check_vma=False,
    )
```

time: 279 us -> 222 us (0.80)
  the two profiles are of different devices: /device:TPU:66 before, /device:TPU:1 now
where the time goes in v3:
time: 222 us; the launch traced here: 220 us
  waiting for transfers between devices  116 us (52%)
  starting transfers between devices  63.2 us (28%)
  Pallas kernels  37.8 us (17%)
  other arithmetic  3.55 us (2%)
    ppermute x16, waiting for transfers between devices, along_section(): lax.ppermute(value, 'section', [(i, (i + CORES * dy) % count ^ flip) for...  43.7 us
    ppermute x14, waiting for transfers between devices, along_expert(): lax.ppermute(value, 'expert', [(i, (i // NX + dz) % planes * NX + (i % NX...  36.6 us
    all_to_all x4, waiting for transfers between devices, swap_x(): lax.all_to_all(value, 'expert', 0, 0, axis_index_groups=x_groups, tiled=T...  35.2 us
    ppermute x16, starting transfers between devices, along_section(): lax.ppermute(value, 'section', [(i, (i + CORES * dy) % count ^ flip) for...  24.3 us
    ppermute x14, starting transfers between devices, along_expert(): lax.ppermute(value, 'expert', [(i, (i // NX + dz) % planes * NX + (i % NX...  23.3 us
    pallas_call x4, Pallas kernels, expand(): call(functools.partial(up_kernel, held, flip), shape(4, 2, held, units),...  16.2 us
    all_to_all x4, starting transfers between devices, swap_x(): lax.all_to_all(value, 'expert', 0, 0, axis_index_groups=x_groups, tiled=T...  15.6 us
    pallas_call x2, Pallas kernels, contract(): call(functools.partial(down_kernel, held), shape(4, 2, held, width), [SME...  11 us
  transfers between devices with their start and end apart: 34, of which 17 were waited for; matrix products, arithmetic and copies ran while one was open for 0% of the time, Pallas kernels for 17%

profile of v3, /device:TPU:1, one launch (start us, length us, event | category | flops | bytes accessed | tf_op | source)
XLA Modules:
  0.0 220.2 jit_solution(4118577470546981202)
XLA Ops:
  4.9 4.0 %collective-permute-start.1 = (bf16[144,896]{1,0:T(8,128)(2,1)S(1)}, bf16[144,896]{1,0:T(8,128)(2,1)S(1)}, u32[]{:S(2)}, u32[]{:S(2)}) collective-permute-start(bf16[144,896]{1,0:T(8,128)(2,1)S(1)} %pad_maximum_fusion.2.refs_0_), channel_id=1, source_target_pairs={{0,28},{1,29},{2,30},{3,31},{4,0},{5,1},{6,2},{7,3},{8,4},{9,5},{1... | collective-permute-start | bytes 774152 | tf_op jit(solution)/shard_map/ppermute | solution.py:21
  8.9 5.9 %collective-permute-done.refs_0_ = bf16[144,896]{1,0:T(8,128)(2,1)S(1)} collective-permute-done((bf16[144,896]{1,0:T(8,128)(2,1)S(1)}, bf16[144,896]{1,0:T(8,128)(2,1)S(1)}, u32[]{:S(2)}, u32[]{:S(2)}) %collective-permute-start) | collective-permute-done | bytes 258080 | tf_op jit(solution)/shard_map/ppermute | solution.py:21
  17.5 5.0 %collective-permute-done.2.refs_2_ = bf16[144,896]{1,0:T(8,128)(2,1)S(1)} collective-permute-done((bf16[144,896]{1,0:T(8,128)(2,1)S(1)}, bf16[144,896]{1,0:T(8,128)(2,1)S(1)}, u32[]{:S(2)}, u32[]{:S(2)}) %collective-permute-start.2) | collective-permute-done | bytes 258080 | tf_op jit(solution)/shard_map/ppermute | solution.py:21
  25.2 4.0 %collective-permute-done.4.refs_2_ = bf16[144,896]{1,0:T(8,128)(2,1)S(1)} collective-permute-done((bf16[144,896]{1,0:T(8,128)(2,1)S(1)}, bf16[144,896]{1,0:T(8,128)(2,1)S(1)}, u32[]{:S(2)}, u32[]{:S(2)}) %collective-permute-start.4) | collective-permute-done | bytes 258080 | tf_op jit(solution)/shard_map/ppermute | solution.py:21
  32.0 4.0 %all-to-all-start = ((bf16[4,192,896]{2,1,0:T(8,128)(2,1)}), bf16[4,192,896]{2,1,0:T(8,128)(2,1)S(1)}, u32[]{:S(2)}, u32[]{:S(2)}) async-start(bf16[4,192,896]{2,1,0:T(8,128)(2,1)} %get-tuple-element.41), calls=%async_computation | async-start | bytes 2752512 | tf_op jit(solution)/shard_map/all_to_all | solution.py:170
  39.2 11.8 %all-to-all-done.rows_ref = bf16[4,192,896]{2,1,0:T(8,128)(2,1)S(1)} async-done(((bf16[4,192,896]{2,1,0:T(8,128)(2,1)}), bf16[4,192,896]{2,1,0:T(8,128)(2,1)S(1)}, u32[]{:S(2)}, u32[]{:S(2)}) %all-to-all-start) | async-done | bytes 1376288 | tf_op jit(solution)/shard_map/all_to_all | solution.py:170
  54.5 4.1 %shard_map.67 = bf16[4,2,96,1024]{3,2,1,0:T(8,128)(2,1)S(1)} custom-call(s32[3]{0:T(128)S(1)} %pad_add_fusion.at_ref, bf16[4,192,896]{2,1,0:T(8,128)(2,1)S(1)} %all-to-all-done.rows_ref, bf16[2,896,1024]{2,1,0:T(8,128)(2,1)} %gate_ref.7, bf16[2,896,1024]{2,1,0:T(8,128)(2,1)} %up_ref.7), custom_call_target="tpu_custom_call" | custom-call | flops 22548578304 | bytes 100663296 | tf_op jit(solution)/shard_map/pallas_call | solution.py:199
  58.6 4.7 %collective-permute-start.7 = (bf16[4,2,96,1024]{3,2,1,0:T(8,128)(2,1)S(1)}, bf16[4,2,96,1024]{3,2,1,0:T(8,128)(2,1)S(1)}, u32[]{:S(2)}, u32[]{:S(2)}) collective-permute-start(bf16[4,2,96,1024]{3,2,1,0:T(8,128)(2,1)S(1)} %shard_map.67), channel_id=1, source_target_pairs={{0,32},{32,0},{64,96},{96,64},{128,160},{160,128},{192,224},{224,1... | collective-permute-start | bytes 4718600 | tf_op jit(solution)/shard_map/ppermute | solution.py:30
  63.3 4.1 %shard_map.66.keep_ref = bf16[4,2,96,1024]{3,2,1,0:T(8,128)(2,1)S(1)} custom-call(s32[3]{0:T(128)S(1)} %pad_add_fusion.at_ref, bf16[4,192,896]{2,1,0:T(8,128)(2,1)S(1)} %all-to-all-done.rows_ref, bf16[2,896,1024]{2,1,0:T(8,128)(2,1)} %gate_ref.7, bf16[2,896,1024]{2,1,0:T(8,128)(2,1)} %up_ref.7), custom_call_target="tpu_custom_call" | custom-call | flops 22548578304 | bytes 100663296 | tf_op jit(solution)/shard_map/pallas_call | solution.py:199
  72.9 4.1 %shard_map.70 = bf16[4,2,96,1024]{3,2,1,0:T(8,128)(2,1)S(1)} custom-call(s32[3]{0:T(128)S(1)} %pad_add_fusion.at_ref, bf16[4,192,896]{2,1,0:T(8,128)(2,1)S(1)} %all-to-all-done.1.rows_ref, bf16[2,896,1024]{2,1,0:T(8,128)(2,1)} %gate_ref.7, bf16[2,896,1024]{2,1,0:T(8,128)(2,1)} %up_ref.7), custom_call_target="tpu_custom_call" | custom-call | flops 22548578304 | bytes 100663296 | tf_op jit(solution)/shard_map/pallas_call | solution.py:199
  78.2 4.1 %shard_map.69.keep_ref = bf16[4,2,96,1024]{3,2,1,0:T(8,128)(2,1)S(1)} custom-call(s32[3]{0:T(128)S(1)} %pad_add_fusion.at_ref, bf16[4,192,896]{2,1,0:T(8,128)(2,1)S(1)} %all-to-all-done.1.rows_ref, bf16[2,896,1024]{2,1,0:T(8,128)(2,1)} %gate_ref.7, bf16[2,896,1024]{2,1,0:T(8,128)(2,1)} %up_ref.7), custom_call_target="tpu_custom_call" | custom-call | flops 22548578304 | bytes 100663296 | tf_op jit(solution)/shard_map/pallas_call | solution.py:199
  82.7 5.7 %collective-permute-done.10.d_ref = bf16[2,96,1024]{2,1,0:T(8,128)(2,1)S(1)} collective-permute-done((bf16[2,96,1024]{2,1,0:T(8,128)(2,1)}, bf16[2,96,1024]{2,1,0:T(8,128)(2,1)S(1)}, u32[]{:S(2)}, u32[]{:S(2)}) %collective-permute-start.10) | collective-permute-done | bytes 393248 | tf_op jit(solution)/shard_map/ppermute | solution.py:30
  94.5 4.6 %collective-permute-done.12 = bf16[96,1024]{1,0:T(8,128)(2,1)S(1)} collective-permute-done((bf16[96,1024]{1,0:T(8,128)(2,1)S(1)}, bf16[96,1024]{1,0:T(8,128)(2,1)S(1)}, u32[]{:S(2)}, u32[]{:S(2)}) %collective-permute-start.12) | collective-permute-done | bytes 196640 | tf_op jit(solution)/shard_map/ppermute | solution.py:30
  108.7 8.6 %collective-permute-done.20.b_ref = bf16[2,96,1024]{2,1,0:T(8,128)(2,1)S(1)} collective-permute-done((bf16[2,96,1024]{2,1,0:T(8,128)(2,1)S(1)}, bf16[2,96,1024]{2,1,0:T(8,128)(2,1)S(1)}, u32[]{:S(2)}, u32[]{:S(2)}) %collective-permute-start.20) | collective-permute-done | bytes 393248 | tf_op jit(solution)/shard_map/ppermute | solution.py:30
  117.3 9.0 %collective-permute-done.21.c_ref = bf16[2,96,1024]{2,1,0:T(8,128)(2,1)S(1)} collective-permute-done((bf16[2,96,1024]{2,1,0:T(8,128)(2,1)S(1)}, bf16[2,96,1024]{2,1,0:T(8,128)(2,1)S(1)}, u32[]{:S(2)}, u32[]{:S(2)}) %collective-permute-start.21) | collective-permute-done | bytes 393248 | tf_op jit(solution)/shard_map/ppermute | solution.py:30
  127.0 3.6 %collective-permute-start.24 = (bf16[96,1024]{1,0:T(8,128)(2,1)S(1)}, bf16[96,1024]{1,0:T(8,128)(2,1)S(1)}, u32[]{:S(2)}, u32[]{:S(2)}) collective-permute-start(bf16[96,1024]{1,0:T(8,128)(2,1)S(1)} %shard_map.75), channel_id=1, source_target_pairs={{0,128},{32,160},{64,192},{96,224},{128,0},{160,32},{192,64},{224,... | collective-permute-start | bytes 589832 | tf_op jit(solution)/shard_map/ppermute | solution.py:30
  133.6 5.8 %collective-permute-done.24 = bf16[96,1024]{1,0:T(8,128)(2,1)S(1)} collective-permute-done((bf16[96,1024]{1,0:T(8,128)(2,1)S(1)}, bf16[96,1024]{1,0:T(8,128)(2,1)S(1)}, u32[]{:S(2)}, u32[]{:S(2)}) %collective-permute-start.24) | collective-permute-done | bytes 196640 | tf_op jit(solution)/shard_map/ppermute | solution.py:30
  141.1 5.1 %shard_map.73 = bf16[4,2,96,896]{3,2,1,0:T(8,128)(2,1)} custom-call(s32[3]{0:T(128)S(1)} %pad_add_fusion.at_ref, bf16[4,96,1024]{2,1,0:T(8,128)(2,1)S(1)} %pad_maximum_fusion.own_ref, bf16[4,96,1024]{2,1,0:T(8,128)(2,1)S(1)} %collective-permute-done.15.other_ref, bf16[2,1024,896]{2,1,0:T(8,128)(2,1)} %down_ref.3), custom_call_target="tpu_custom_call" | custom-call | flops 22548578304 | bytes 100663296 | tf_op jit(solution)/shard_map/pallas_call | solution.py:223
  146.2 4.5 %all-to-all-start.2 = ((bf16[4,2,96,896]{3,2,1,0:T(8,128)(2,1)}), bf16[4,2,96,896]{3,2,1,0:T(8,128)(2,1)S(1)}, u32[]{:S(2)}, u32[]{:S(2)}) async-start(bf16[4,2,96,896]{3,2,1,0:T(8,128)(2,1)} %shard_map.73), calls=%async_computation.2 | async-start | bytes 2752512 | tf_op jit(solution)/shard_map/all_to_all | solution.py:170
  150.7 5.8 %shard_map.76 = bf16[4,2,96,896]{3,2,1,0:T(8,128)(2,1)} custom-call(s32[3]{0:T(128)S(1)} %pad_add_fusion.at_ref, bf16[4,96,1024]{2,1,0:T(8,128)(2,1)S(1)} %pad_maximum_fusion.1.own_ref, bf16[4,96,1024]{2,1,0:T(8,128)(2,1)} %collective-permute-done.26.other_ref, bf16[2,1024,896]{2,1,0:T(8,128)(2,1)} %down_ref.3), custom_call_target="tpu_custom_call" | custom-call | flops 22548578304 | bytes 100663296 | tf_op jit(solution)/shard_map/pallas_call | solution.py:223
  156.6 12.6 %all-to-all-done.2.back_ref = bf16[4,2,96,896]{3,2,1,0:T(8,128)(2,1)S(1)} async-done(((bf16[4,2,96,896]{3,2,1,0:T(8,128)(2,1)}), bf16[4,2,96,896]{3,2,1,0:T(8,128)(2,1)S(1)}, u32[]{:S(2)}, u32[]{:S(2)}) %all-to-all-start.2) | async-done | bytes 1376288 | tf_op jit(solution)/shard_map/all_to_all | solution.py:170
  179.4 10.8 %all-to-all-done.3.back_ref = bf16[4,2,96,896]{3,2,1,0:T(8,128)(2,1)S(1)} async-done(((bf16[4,2,96,896]{3,2,1,0:T(8,128)(2,1)}), bf16[4,2,96,896]{3,2,1,0:T(8,128)(2,1)S(1)}, u32[]{:S(2)}, u32[]{:S(2)}) %all-to-all-start.3) | async-done | bytes 1376288 | tf_op jit(solution)/shard_map/all_to_all | solution.py:170
  197.6 12.9 %collective-permute-done.27 = bf16[128,896]{1,0:T(8,128)(2,1)S(1)} collective-permute-done((bf16[128,896]{1,0:T(8,128)(2,1)S(1)}, bf16[128,896]{1,0:T(8,128)(2,1)S(1)}, u32[]{:S(2)}, u32[]{:S(2)}) %collective-permute-start.27) | collective-permute-done | bytes 229408 | tf_op jit(solution)/shard_map/ppermute | solution.py:21
  210.5 8.8 %collective-permute-done.28 = bf16[128,896]{1,0:T(8,128)(2,1)S(1)} collective-permute-done((bf16[128,896]{1,0:T(8,128)(2,1)S(1)}, bf16[128,896]{1,0:T(8,128)(2,1)S(1)}, u32[]{:S(2)}, u32[]{:S(2)}) %collective-permute-start.28) | collective-permute-done | bytes 229408 | tf_op jit(solution)/shard_map/ppermute | solution.py:21
  (66 shorter events, 66.5 us)
Async XLA Ops:
  2.4 12.4 %collective-permute-start = (bf16[144,896]{1,0:T(8,128)(2,1)S(1)}, bf16[144,896]{1,0:T(8,128)(2,1)S(1)}, u32[]{:S(2)}, u32[]{:S(2)}) collective-permute-start(bf16[144,896]{1,0:T(8,128)(2,1)S(1)} %pad_maximum_fusion.2.refs_0_), channel_id=1, source_target_pairs={{0,4},{1,5},{2,6},{3,7},{4,8},{5,9},{6,10},{7,11},{8,12},{9,13},{1... | collective-permute-start | bytes 774152 | tf_op jit(solution)/shard_map/ppermute | solution.py:21
  4.9 9.9 %collective-permute-start.1 = (bf16[144,896]{1,0:T(8,128)(2,1)S(1)}, bf16[144,896]{1,0:T(8,128)(2,1)S(1)}, u32[]{:S(2)}, u32[]{:S(2)}) collective-permute-start(bf16[144,896]{1,0:T(8,128)(2,1)S(1)} %pad_maximum_fusion.2.refs_0_), channel_id=1, source_target_pairs={{0,28},{1,29},{2,30},{3,31},{4,0},{5,1},{6,2},{7,3},{8,4},{9,5},{1... | collective-permute-start | bytes 774152 | tf_op jit(solution)/shard_map/ppermute | solution.py:21
  22.6 13.4 %collective-permute-start.6 = (bf16[144,896]{1,0:T(8,128)(2,1)S(1)}, bf16[144,896]{1,0:T(8,128)(2,1)S(1)}, u32[]{:S(2)}, u32[]{:S(2)}) collective-permute-start(bf16[144,896]{1,0:T(8,128)(2,1)S(1)} %collective-permute-done.3.refs_3_), channel_id=1, source_target_pairs={{0,28},{1,29},{2,30},{3,31},{4,0},{5,1},{6,2},{7,3},{8,4},{9,5},{1... | collective-permute-start | bytes 774152 | tf_op jit(solution)/shard_map/ppermute | solution.py:21
  32.0 19.0 %all-to-all-start = ((bf16[4,192,896]{2,1,0:T(8,128)(2,1)}), bf16[4,192,896]{2,1,0:T(8,128)(2,1)S(1)}, u32[]{:S(2)}, u32[]{:S(2)}) async-start(bf16[4,192,896]{2,1,0:T(8,128)(2,1)} %get-tuple-element.41), calls=%async_computation | async-start | bytes 2752512 | tf_op jit(solution)/shard_map/all_to_all | solution.py:170
  51.0 21.9 %all-to-all-start.1 = ((bf16[4,192,896]{2,1,0:T(8,128)(2,1)}), bf16[4,192,896]{2,1,0:T(8,128)(2,1)S(1)}, u32[]{:S(2)}, u32[]{:S(2)}) async-start(bf16[4,192,896]{2,1,0:T(8,128)(2,1)} %get-tuple-element.44), calls=%async_computation.1 | async-start | bytes 2752512 | tf_op jit(solution)/shard_map/all_to_all | solution.py:170
  68.5 19.9 %collective-permute-start.10 = (bf16[2,96,1024]{2,1,0:T(8,128)(2,1)}, bf16[2,96,1024]{2,1,0:T(8,128)(2,1)S(1)}, u32[]{:S(2)}, u32[]{:S(2)}) collective-permute-start(bf16[2,96,1024]{2,1,0:T(8,128)(2,1)} %get-tuple-element.51), channel_id=1, source_target_pairs={{0,192},{32,224},{64,0},{96,32},{128,64},{160,96},{192,128},{224,1... | collective-permute-start | bytes 1179656 | tf_op jit(solution)/shard_map/ppermute | solution.py:30
  71.3 20.3 %collective-permute-start.8 = (bf16[2,96,1024]{2,1,0:T(8,128)(2,1)}, bf16[2,96,1024]{2,1,0:T(8,128)(2,1)S(1)}, u32[]{:S(2)}, u32[]{:S(2)}) collective-permute-start(bf16[2,96,1024]{2,1,0:T(8,128)(2,1)} %get-tuple-element.49), channel_id=1, source_target_pairs={{0,64},{32,96},{64,128},{96,160},{128,192},{160,224},{192,0},{224,... | collective-permute-start | bytes 1179656 | tf_op jit(solution)/shard_map/ppermute | solution.py:30
  71.3 20.3 %collective-permute-start.9 = (bf16[2,96,1024]{2,1,0:T(8,128)(2,1)S(1)}, bf16[2,96,1024]{2,1,0:T(8,128)(2,1)S(1)}, u32[]{:S(2)}, u32[]{:S(2)}) collective-permute-start(bf16[2,96,1024]{2,1,0:T(8,128)(2,1)S(1)} %get-tuple-element.50), channel_id=1, source_target_pairs={{0,128},{32,160},{64,192},{96,224},{128,0},{160,32},{192,64},{224,... | collective-permute-start | bytes 1179656 | tf_op jit(solution)/shard_map/ppermute | solution.py:30
  91.9 9.9 %collective-permute-start.13 = (bf16[96,1024]{1,0:T(8,128)(2,1)S(1)}, bf16[96,1024]{1,0:T(8,128)(2,1)S(1)}, u32[]{:S(2)}, u32[]{:S(2)}) collective-permute-start(bf16[96,1024]{1,0:T(8,128)(2,1)S(1)} %shard_map.72), channel_id=1, source_target_pairs={{0,128},{32,160},{64,192},{96,224},{128,0},{160,32},{192,64},{224,... | collective-permute-start | bytes 589832 | tf_op jit(solution)/shard_map/ppermute | solution.py:30
  103.1 38.0 %collective-permute-start.15 = (bf16[4,96,1024]{2,1,0:T(8,128)(2,1)S(1)}, bf16[4,96,1024]{2,1,0:T(8,128)(2,1)S(1)}, u32[]{:S(2)}, u32[]{:S(2)}) collective-permute-start(bf16[4,96,1024]{2,1,0:T(8,128)(2,1)S(1)} %pad_maximum_fusion.own_ref), channel_id=1, source_target_pairs={{0,32},{32,0},{64,96},{96,64},{128,160},{160,128},{192,224},{224,1... | collective-permute-start | bytes 2359304 | tf_op jit(solution)/shard_map/ppermute | solution.py:30
  105.4 11.9 %collective-permute-start.20 = (bf16[2,96,1024]{2,1,0:T(8,128)(2,1)S(1)}, bf16[2,96,1024]{2,1,0:T(8,128)(2,1)S(1)}, u32[]{:S(2)}, u32[]{:S(2)}) collective-permute-start(bf16[2,96,1024]{2,1,0:T(8,128)(2,1)S(1)} %get-tuple-element.68), channel_id=1, source_target_pairs={{0,64},{32,96},{64,128},{96,160},{128,192},{160,224},{192,0},{224,... | collective-permute-start | bytes 1179656 | tf_op jit(solution)/shard_map/ppermute | solution.py:30
  105.4 20.9 %collective-permute-start.21 = (bf16[2,96,1024]{2,1,0:T(8,128)(2,1)S(1)}, bf16[2,96,1024]{2,1,0:T(8,128)(2,1)S(1)}, u32[]{:S(2)}, u32[]{:S(2)}) collective-permute-start(bf16[2,96,1024]{2,1,0:T(8,128)(2,1)S(1)} %get-tuple-element.69), channel_id=1, source_target_pairs={{0,128},{32,160},{64,192},{96,224},{128,0},{160,32},{192,64},{224,... | collective-permute-start | bytes 1179656 | tf_op jit(solution)/shard_map/ppermute | solution.py:30
  108.7 17.6 %collective-permute-start.22 = (bf16[2,96,1024]{2,1,0:T(8,128)(2,1)S(1)}, bf16[2,96,1024]{2,1,0:T(8,128)(2,1)S(1)}, u32[]{:S(2)}, u32[]{:S(2)}) collective-permute-start(bf16[2,96,1024]{2,1,0:T(8,128)(2,1)S(1)} %get-tuple-element.70), channel_id=1, source_target_pairs={{0,192},{32,224},{64,0},{96,32},{128,64},{160,96},{192,128},{224,1... | collective-permute-start | bytes 1179656 | tf_op jit(solution)/shard_map/ppermute | solution.py:30
  127.0 12.3 %collective-permute-start.24 = (bf16[96,1024]{1,0:T(8,128)(2,1)S(1)}, bf16[96,1024]{1,0:T(8,128)(2,1)S(1)}, u32[]{:S(2)}, u32[]{:S(2)}) collective-permute-start(bf16[96,1024]{1,0:T(8,128)(2,1)S(1)} %shard_map.75), channel_id=1, source_target_pairs={{0,128},{32,160},{64,192},{96,224},{128,0},{160,32},{192,64},{224,... | collective-permute-start | bytes 589832 | tf_op jit(solution)/shard_map/ppermute | solution.py:30
  139.5 11.3 %collective-permute-start.26 = (bf16[4,96,1024]{2,1,0:T(8,128)(2,1)S(1)}, bf16[4,96,1024]{2,1,0:T(8,128)(2,1)}, u32[]{:S(2)}, u32[]{:S(2)}) collective-permute-start(bf16[4,96,1024]{2,1,0:T(8,128)(2,1)S(1)} %pad_maximum_fusion.1.own_ref), channel_id=1, source_target_pairs={{0,32},{32,0},{64,96},{96,64},{128,160},{160,128},{192,224},{224,1... | collective-permute-start | bytes 2359304 | tf_op jit(solution)/shard_map/ppermute | solution.py:30
  146.2 22.9 %all-to-all-start.2 = ((bf16[4,2,96,896]{3,2,1,0:T(8,128)(2,1)}), bf16[4,2,96,896]{3,2,1,0:T(8,128)(2,1)S(1)}, u32[]{:S(2)}, u32[]{:S(2)}) async-start(bf16[4,2,96,896]{3,2,1,0:T(8,128)(2,1)} %shard_map.73), calls=%async_computation.2 | async-start | bytes 2752512 | tf_op jit(solution)/shard_map/all_to_all | solution.py:170
  169.2 21.0 %all-to-all-start.3 = ((bf16[4,2,96,896]{3,2,1,0:T(8,128)(2,1)}), bf16[4,2,96,896]{3,2,1,0:T(8,128)(2,1)S(1)}, u32[]{:S(2)}, u32[]{:S(2)}) async-start(bf16[4,2,96,896]{3,2,1,0:T(8,128)(2,1)} %shard_map.76), calls=%async_computation.3 | async-start | bytes 2752512 | tf_op jit(solution)/shard_map/all_to_all | solution.py:170
  174.3 20.0 %collective-permute-start.16 = (bf16[128,896]{1,0:T(8,128)(2,1)}, bf16[128,896]{1,0:T(8,128)(2,1)S(1)}, u32[]{:S(2)}, u32[]{:S(2)}) collective-permute-start(bf16[128,896]{1,0:T(8,128)(2,1)} %get-tuple-element.63), channel_id=1, source_target_pairs={{0,28},{1,29},{2,30},{3,31},{4,0},{5,1},{6,2},{7,3},{8,4},{9,5},{1... | collective-permute-start | bytes 688136 | tf_op jit(solution)/shard_map/ppermute | solution.py:21
  177.0 17.6 %collective-permute-start.17 = (bf16[128,896]{1,0:T(8,128)(2,1)S(1)}, bf16[128,896]{1,0:T(8,128)(2,1)S(1)}, u32[]{:S(2)}, u32[]{:S(2)}) collective-permute-start(bf16[128,896]{1,0:T(8,128)(2,1)S(1)} %get-tuple-element.64), channel_id=1, source_target_pairs={{0,4},{1,5},{2,6},{3,7},{4,8},{5,9},{6,10},{7,11},{8,12},{9,13},{1... | collective-permute-start | bytes 688136 | tf_op jit(solution)/shard_map/ppermute | solution.py:21
  177.0 20.6 %collective-permute-start.18 = (bf16[128,896]{1,0:T(8,128)(2,1)S(1)}, bf16[128,896]{1,0:T(8,128)(2,1)S(1)}, u32[]{:S(2)}, u32[]{:S(2)}) collective-permute-start(bf16[128,896]{1,0:T(8,128)(2,1)S(1)} %get-tuple-element.65), channel_id=1, source_target_pairs={{0,24},{1,25},{2,26},{3,27},{4,28},{5,29},{6,30},{7,31},{8,0},{9,1... | collective-permute-start | bytes 688136 | tf_op jit(solution)/shard_map/ppermute | solution.py:21
  178.2 19.4 %collective-permute-start.19 = (bf16[128,896]{1,0:T(8,128)(2,1)S(1)}, bf16[128,896]{1,0:T(8,128)(2,1)S(1)}, u32[]{:S(2)}, u32[]{:S(2)}) collective-permute-start(bf16[128,896]{1,0:T(8,128)(2,1)S(1)} %get-tuple-element.66), channel_id=1, source_target_pairs={{0,8},{1,9},{2,10},{3,11},{4,12},{5,13},{6,14},{7,15},{8,16},{9,17... | collective-permute-start | bytes 688136 | tf_op jit(solution)/shard_map/ppermute | solution.py:21
  191.2 19.3 %collective-permute-start.27 = (bf16[128,896]{1,0:T(8,128)(2,1)S(1)}, bf16[128,896]{1,0:T(8,128)(2,1)S(1)}, u32[]{:S(2)}, u32[]{:S(2)}) collective-permute-start(bf16[128,896]{1,0:T(8,128)(2,1)S(1)} %get-tuple-element.74), channel_id=1, source_target_pairs={{0,16},{1,17},{2,18},{3,19},{4,20},{5,21},{6,22},{7,23},{8,24},{9,... | collective-permute-start | bytes 688136 | tf_op jit(solution)/shard_map/ppermute | solution.py:21
  194.3 25.0 %collective-permute-start.28 = (bf16[128,896]{1,0:T(8,128)(2,1)S(1)}, bf16[128,896]{1,0:T(8,128)(2,1)S(1)}, u32[]{:S(2)}, u32[]{:S(2)}) collective-permute-start(bf16[128,896]{1,0:T(8,128)(2,1)S(1)} %get-tuple-element.75), channel_id=1, source_target_pairs={{0,20},{1,21},{2,22},{3,23},{4,24},{5,25},{6,26},{7,27},{8,28},{9,... | collective-permute-start | bytes 688136 | tf_op jit(solution)/shard_map/ppermute | solution.py:21
  194.6 24.7 %collective-permute-start.29 = (bf16[128,896]{1,0:T(8,128)(2,1)S(1)}, bf16[128,896]{1,0:T(8,128)(2,1)S(1)}, u32[]{:S(2)}, u32[]{:S(2)}) collective-permute-start(bf16[128,896]{1,0:T(8,128)(2,1)S(1)} %get-tuple-element.76), channel_id=1, source_target_pairs={{0,12},{1,13},{2,14},{3,15},{4,16},{5,17},{6,18},{7,19},{8,20},{9,... | collective-permute-start | bytes 688136 | tf_op jit(solution)/shard_map/ppermute | solution.py:21
  (10 other events, 75.9 us)
